TPU v7x, 32 devices: a whole 2x2x4 slice. The times are simulated.
32 devices in a mesh: space: 8 (over y, x, core), mode: 4 (over z).
Axes of the slice: x: 2, y: 2, z: 4, core: 2. Of those that a mesh axis runs over, the one named last changes fastest.
Arguments:
- mode_fields: float32 [3, 128, 8, 512], P(None, 'mode', 'space'), may hold values from -2.5 to 2.5
- volume: float32 [8, 512], P('space'), may hold values from 0.25 to 4
- fluid_mask: int32 [8, 512], P('space'), may hold values 0 or 1
Outputs:
- convection: float32 [128, 128, 128], P('space', None, 'mode')
All inputs are finite; a program needn't handle non-finite values. No bound on the sum of `fluid_mask` on one device may be relied on, other than what follows from the above.
Results may differ from a plain program's by a relative error of at most 0.0001.
Values sent between devices are 32-bit elements; how exact they have to be, the bound alone decides.
No kernel may reach another device: no remote copies, remote signals or barrier semaphores. Data moves between devices by JAX's collectives and lax.ppermute only.
A program may use at most 128 MiB of HBM per device.

v0:
```python
import jax
import jax.numpy as jnp
from jax import lax
from jax.sharding import PartitionSpec as P

M = 128
TGY = 8
TX = 4
TY = 16
TZ = 8


def passed_along(value, axis, by):
    devices = lax.axis_size(axis)
    pairs = [(i, i + by) for i in range(devices) if 0 <= i + by < devices]
    return lax.ppermute(value, axis, pairs)


def derivative(padded, axis, length):

    def shifted(offset):
        return lax.slice_in_dim(padded, 2 + offset, 2 + offset + length, axis=axis)

    return (8.0 * (shifted(1) - shifted(-1)) - (shifted(2) - shifted(-2))) / 12.0


def neighbour(rim_block, offset):
    return passed_along(rim_block, "space", offset)


def per_device(mode_fields, volume, fluid_mask):
    k_count = mode_fields.shape[1]
    cell_count = mode_fields.shape[3]
    rim_rows = 3 * k_count
    own_block = mode_fields.reshape(3, k_count, TX, TY, TZ)
    upper_x = own_block[:, :, TX - 2 :].reshape(rim_rows, 2 * TY * TZ)
    lower_x = own_block[:, :, :2].reshape(rim_rows, 2 * TY * TZ)
    upper_y = own_block[:, :, :, TY - 2 :].reshape(rim_rows, TX * 2 * TZ)
    lower_y = own_block[:, :, :, :2].reshape(rim_rows, TX * 2 * TZ)
    below_x = neighbour(upper_x, TGY).reshape(3, k_count, 2, TY, TZ)
    above_x = neighbour(lower_x, -TGY).reshape(3, k_count, 2, TY, TZ)
    tile_column = lax.axis_index("space") % TGY
    below_y = neighbour(upper_y, 1).reshape(3, k_count, TX, 2, TZ)
    above_y = neighbour(lower_y, -1).reshape(3, k_count, TX, 2, TZ)
    below_y = jnp.where(tile_column > 0, below_y, jnp.zeros_like(below_y))
    above_y = jnp.where(tile_column < TGY - 1, above_y, jnp.zeros_like(above_y))
    padded_x = jnp.concatenate([below_x, own_block, above_x], axis=2)
    padded_y = jnp.concatenate([below_y, own_block, above_y], axis=3)
    padded_z = jnp.pad(own_block, ((0, 0), (0, 0), (0, 0), (0, 0), (2, 2)))
    gradient = jnp.stack(
        [derivative(padded_x, 2, TX), derivative(padded_y, 3, TY), derivative(padded_z, 4, TZ)]
    )
    gradient = gradient.reshape(3, 3, k_count, cell_count)
    weights = (volume * fluid_mask.astype(jnp.float32)).reshape(cell_count)
    own_fields = mode_fields.reshape(3, k_count, cell_count)
    everything = lax.all_gather(own_fields, "mode", axis=1, tiled=True)
    weighted = everything * weights
    block_width = min(64, M)
    pieces = []
    for block_start in range(0, M, block_width):
        advected = jnp.einsum(
            "ejc,edkc->djkc",
            everything[:, block_start : block_start + block_width],
            gradient,
            precision=lax.Precision.HIGHEST,
        )
        pieces.append(
            jnp.einsum("dic,djkc->ijk", weighted, advected, precision=lax.Precision.HIGHEST)
        )
    partial_tensor = jnp.concatenate(pieces, axis=1)
    return lax.psum_scatter(partial_tensor, "space", scatter_dimension=0, tiled=True)


def solution(mesh):
    in_specs = (P(None, "mode", "space", None), P("space", None), P("space", None))
    out_specs = P("space", None, "mode")
    return jax.shard_map(
        per_device, mesh=mesh, in_specs=in_specs, out_specs=out_specs, check_vma=False
    )
```

profile of v0, /device:TPU:0, one launch (start us, length us, event | category | flops | bytes accessed | tf_op | source)
XLA Modules:
  0.0 282.0 jit_solution(13994162016988459464)
XLA Ops:
  6.5 0.0 reduce-scatter.2.cloned.1.call-start
  6.5 1.2 copy.77
  7.7 0.0 copy-start.1
  7.8 0.1 copy.82
  7.8 0.7 reshape.46
  8.6 1.3 collective-permute-start.2
  9.9 0.1 copy.84
  9.9 0.7 reshape.47
  10.7 3.6 %collective-permute-start.3 = (f32[96,64]{0,1:T(8,128)}, f32[96,64]{0,1:T(8,128)}, u32[]{:S(2)}, u32[]{:S(2)}) collective-permute-start(f32[96,64]{0,1:T(8,128)} %reshape.47), channel_id=1, source_target_pairs={{0,4},{4,8},{8,12},{12,16},{16,20},{20,24},{24,28},{1,5},{5,9},{9,... | collective-permute-start | bytes 73736 | tf_op jit(solution)/shard_map/ppermute | solution.py:16
  14.3 0.1 fusion.37
  14.3 0.3 copy.78
  14.6 0.2 reshape.42
  14.8 0.0 copy-start.3
  14.9 1.3 collective-permute-start
  16.2 0.3 copy.80
  16.4 0.9 reshape.44
  17.3 1.3 collective-permute-start.1
  18.7 21.2 %all-gather = f32[3,128,1,512]{3,2,0,1:T(1,128)S(1)} all-gather(f32[3,32,1,512]{3,2,0,1:T(1,128)S(1)} %copy.75), channel_id=2, replica_groups=mesh['space'=8,'mode'=4] {'mode'}, dimensions={1}, use_global_device_ids=true | all-gather | bytes 983040 | tf_op jit(solution)/shard_map/all_gather | solution.py:56
  39.9 0.1 copy.117
  40.0 0.1 slice_bitcast_fusion.1
  40.0 0.0 copy-done.2
  40.0 0.0 copy-done.3
  40.1 0.4 copy.94
  40.5 1.3 copy.96
  41.8 0.0 collective-permute-done.2
  41.8 0.8 broadcast_select_fusion.1
  42.6 0.0 collective-permute-done.3
  42.6 0.1 select_n.30
  42.7 0.6 copy.83
  43.3 0.1 select_n.33
  43.5 0.6 copy.85
  44.1 0.0 collective-permute-done
  44.1 1.1 reshape.43
  45.3 0.0 collective-permute-done.1
  45.3 1.1 reshape.45
  46.4 2.2 fusion.20
  48.6 0.0 copy-start
  48.6 0.8 copy.86
  49.4 0.8 copy.87
  50.2 0.8 copy.88
  51.1 43.6 %convolution_bitcast_fusion = f32[3,64,32,512]{1,2,0,3:T(8,128)} fusion(f32[3,64,512,1]{1,0,3,2:T(4,128)S(1)} %copy-done, f32[1,3,32,512]{2,0,1,3:T(1,128)S(1)} %copy.88, f32[1,3,32,512]{2,0,1,3:T(1,128)S(1)} %copy.87, f32[1,3,32,512]{2,0,1,3:T(1,128)S(1)} %copy.86), kind=kOutput, calls=%fused_computation.4 | convolution fusion | flops 113541120 | bytes 13565952 | tf_op jit(solution)/shard_map/ejc,edkc->djkc/dot_general | solution.py:61
  94.7 43.6 %convolution_bitcast_fusion.1 = f32[3,64,32,512]{1,2,0,3:T(8,128)} fusion(f32[3,64,512,1]{1,0,3,2:T(4,128)S(1)} %copy.94, f32[1,3,32,512]{2,0,1,3:T(1,128)S(1)} %copy.88, f32[1,3,32,512]{2,0,1,3:T(1,128)S(1)} %copy.87, f32[1,3,32,512]{2,0,1,3:T(1,128)S(1)} %copy.86), kind=kOutput, calls=%fused_computation.5 | convolution fusion | flops 113541120 | bytes 13565952 | tf_op jit(solution)/shard_map/ejc,edkc->djkc/dot_general | solution.py:61
  138.3 46.4 %fusion.7 = f32[128,64,32]{0,1,2:T(8,128)S(1)} fusion(f32[3,64,32,512]{1,2,0,3:T(8,128)} %convolution_bitcast_fusion, f32[512]{0:T(512)S(1)} %bitcast.60, f32[3,128,1,512]{3,2,0,1:T(1,128)S(1)} %all-gather), kind=kOutput, calls=%fused_computation.13 | convolution fusion | flops 4832034816 | bytes 14419968 | tf_op jit(solution)/shard_map/dic,djkc->ijk/dot_general | solution.py:68
  184.8 46.3 %fusion.4 = f32[128,64,32]{0,1,2:T(8,128)S(1)} fusion(f32[3,64,32,512]{1,2,0,3:T(8,128)} %convolution_bitcast_fusion.1, f32[512]{0:T(512)S(1)} %bitcast.61, f32[3,128,1,512]{3,2,0,1:T(1,128)S(1)} %all-gather), kind=kOutput, calls=%fused_computation.12 | convolution fusion | flops 4832034816 | bytes 14419968 | tf_op jit(solution)/shard_map/dic,djkc->ijk/dot_general | solution.py:68
  231.1 0.1 pad_maximum_fusion.1
  231.2 2.1 copy.93
  233.3 0.0 reduce-scatter.2.cloned.1.call-update
  233.3 41.6 %reduce-scatter.2.cloned.1.call-done = f32[16,128,32]{1,2,0:T(8,128)} async-done(((f32[128,128,32]{1,2,0:T(8,128)}), f32[16,128,32]{1,2,0:T(8,128)}) %reduce-scatter.2.cloned.1.call-update) | async-done | bytes 262160 | tf_op jit(solution)/shard_map/reduce_scatter | solution.py:71
  (9 shorter events, 0.1 us)
Async XLA Ops:
  6.5 268.4 %reduce-scatter.2.cloned.1.call-start = ((), (), s32[]{:S(2)}) async-start(), calls=%async_computation.1 | async-start | bytes 2359296 | tf_op jit(solution)/shard_map/reduce_scatter | solution.py:71
  7.7 10.9 %copy-start.1 = (f32[3,32,1,512]{3,2,1,0:T(1,128)S(1)}, f32[3,32,1,512]{3,2,1,0:T(1,128)}, u32[]{:S(2)}) copy-start(f32[3,32,1,512]{3,2,1,0:T(1,128)} %param.3) | copy-start | bytes 589828
  8.6 33.2 %collective-permute-start.2 = (f32[96,64]{0,1:T(8,128)}, f32[96,64]{0,1:T(8,128)}, u32[]{:S(2)}, u32[]{:S(2)}) collective-permute-start(f32[96,64]{0,1:T(8,128)} %reshape.46), channel_id=1, source_target_pairs={{4,0},{8,4},{12,8},{16,12},{20,16},{24,20},{28,24},{5,1},{9,5},{13... | collective-permute-start | bytes 73736 | tf_op jit(solution)/shard_map/ppermute | solution.py:16
  10.7 31.9 %collective-permute-start.3 = (f32[96,64]{0,1:T(8,128)}, f32[96,64]{0,1:T(8,128)}, u32[]{:S(2)}, u32[]{:S(2)}) collective-permute-start(f32[96,64]{0,1:T(8,128)} %reshape.47), channel_id=1, source_target_pairs={{0,4},{4,8},{8,12},{12,16},{16,20},{20,24},{24,28},{1,5},{5,9},{9,... | collective-permute-start | bytes 73736 | tf_op jit(solution)/shard_map/ppermute | solution.py:16
  14.8 25.2 %copy-start.2 = (f32[1,512]{1,0:T(1,128)S(1)}, f32[1,512]{1,0:T(1,128)}, u32[]{:S(2)}) copy-start(f32[1,512]{1,0:T(1,128)} %param.4) | copy-start | bytes 6148
  14.8 25.2 %copy-start.3 = (s32[1,512]{1,0:T(1,128)S(1)}, s32[1,512]{1,0:T(1,128)}, u32[]{:S(2)}) copy-start(s32[1,512]{1,0:T(1,128)} %param.5) | copy-start | bytes 6148
  14.9 29.2 %collective-permute-start = (f32[96,256]{0,1:T(8,128)S(1)}, f32[96,256]{0,1:T(8,128)}, u32[]{:S(2)}, u32[]{:S(2)}) collective-permute-start(f32[96,256]{0,1:T(8,128)S(1)} %reshape.42), channel_id=1, source_target_pairs={} | collective-permute-start | bytes 294920 | tf_op jit(solution)/shard_map/ppermute | solution.py:16
  17.3 27.9 %collective-permute-start.1 = (f32[96,256]{0,1:T(8,128)}, f32[96,256]{0,1:T(8,128)}, u32[]{:S(2)}, u32[]{:S(2)}) collective-permute-start(f32[96,256]{0,1:T(8,128)} %reshape.44), channel_id=1, source_target_pairs={} | collective-permute-start | bytes 294920 | tf_op jit(solution)/shard_map/ppermute | solution.py:16
  48.6 2.5 copy-start
Sparse Core Ops, SparseCore 0:
  233.4 41.4 reduce-scatter.1
where the time goes:
time: 287 us; the launch traced here: 282 us
  matrix products  180 us (63%)
  waiting for transfers between devices  41.7 us (15%)
  blocking collectives  21.2 us (7%)
  local copies, waits for them, and re-layouts  14.7 us (5%)
  between operations  13.9 us (5%)
  starting transfers between devices  7.52 us (3%)
  other arithmetic  3.07 us (1%)
    dot_general x2, matrix products, per_device(): jnp.einsum('dic,djkc->ijk', weighted, advected, precision=lax.Precision.H...  92.7 us
    dot_general x2, matrix products, per_device(): jnp.einsum('ejc,edkc->djkc', everything[:, block_start:block_start + bloc...  87.2 us
    reduce_scatter x1, waiting for transfers between devices, per_device(): lax.psum_scatter(partial_tensor, 'space', scatter_dimension=0, tiled=True)  41.6 us
    all_gather x1, blocking collectives, per_device(): everything = lax.all_gather(own_fields, 'mode', axis=1, tiled=True)  21.2 us
    ppermute x4, starting transfers between devices, passed_along(): return lax.ppermute(value, axis, pairs)  7.51 us
  transfers between devices with their start and end apart: 5, of which 1 were waited for; matrix products, arithmetic and copies ran while one was open for 3% of the time, Pallas kernels for 0%

commit v1 on v0

--- a/solution.py
+++ b/solution.py
@@ -1,6 +1,10 @@
+import functools
+
 import jax
 import jax.numpy as jnp
 from jax import lax
+from jax.experimental import pallas as pl
+from jax.experimental.pallas import tpu as pltpu
 from jax.sharding import PartitionSpec as P
 
 M = 128
@@ -28,7 +32,7 @@
     return passed_along(rim_block, "space", offset)
 
 
-def per_device(mode_fields, volume, fluid_mask):
+def per_device_general(mode_fields, volume, fluid_mask):
     k_count = mode_fields.shape[1]
     cell_count = mode_fields.shape[3]
     rim_rows = 3 * k_count
@@ -71,9 +75,263 @@
     return lax.psum_scatter(partial_tensor, "space", scatter_dimension=0, tiled=True)
 
 
+LANES = TY * TZ
+CELLS = TX * LANES
+F32 = jnp.float32
+BF16 = jnp.bfloat16
+MIB = 1 << 20
+
+
+def on_chip(kernel, out_shape, scratch=(), flops=0, limit=48):
+    outs = out_shape if isinstance(out_shape, (list, tuple)) else [out_shape]
+
+    def call(*operands):
+        moved = sum(a.size * a.dtype.itemsize for a in list(operands) + list(outs))
+        return pl.pallas_call(
+            kernel,
+            out_shape=out_shape,
+            in_specs=[pl.BlockSpec(memory_space=pltpu.VMEM)] * len(operands),
+            out_specs=jax.tree.map(lambda _: pl.BlockSpec(memory_space=pltpu.VMEM), out_shape),
+            scratch_shapes=list(scratch),
+            compiler_params=pltpu.CompilerParams(vmem_limit_bytes=limit * MIB),
+            cost_estimate=pl.CostEstimate(flops=flops, bytes_accessed=moved, transcendentals=0),
+        )(*operands)
+
+    return call
+
+
+def lane_index(rows):
+    return lax.broadcasted_iota(jnp.int32, (rows, LANES), 1)
+
+
+def rim_kernel(own_ref, rim_ref):
+    rows = rim_ref.shape[0]
+    upper = lax.axis_index("space") % 2 == 1
+    lane = lane_index(rows)
+    width = 2 * TZ
+    total = jnp.zeros((rows, LANES), F32)
+    for x in range(TX):
+        chunk = own_ref[pl.ds(x, rows, stride=TX), :]
+        first = pltpu.roll(chunk, (width * x) % LANES, 1)
+        last = pltpu.roll(chunk, (width * x + width) % LANES, 1)
+        inside = (lane >= width * x) & (lane < width * (x + 1))
+        total = jnp.where(inside, jnp.where(upper, last, first), total)
+    rim_ref[...] = total
+
+
+def gradient_kernel(own_ref, beside_ref, rim_ref, rim_beside_ref, grad_ref):
+    k_count = grad_ref.shape[3]
+    odd = lax.axis_index("space") % 2
+    upper = odd == 1
+    lane = lane_index(k_count)
+    in_z = lane % TZ
+    width = 2 * TZ
+
+    def back(value, by):
+        return pltpu.roll(value, by, 1)
+
+    def ahead(value, by):
+        return pltpu.roll(value, LANES - by, 1)
+
+    def central(plus1, minus1, plus2, minus2):
+        return (8.0 * (plus1 - minus1) - (plus2 - minus2)) / 12.0
+
+    zero = jnp.zeros((k_count, LANES), F32)
+    for d in range(3):
+        start = d * k_count * TX
+        own = [own_ref[pl.ds(start + x, k_count, stride=TX), :] for x in range(TX)]
+        beside = [beside_ref[pl.ds(start + x, k_count, stride=TX), :] for x in range(TX)]
+        rim = rim_ref[pl.ds(d * k_count, k_count), :]
+        rim_beside = rim_beside_ref[pl.ds(d * k_count, k_count), :]
+        low = [jnp.where(upper, b, a) for a, b in zip(own, beside)]
+        high = [jnp.where(upper, a, b) for a, b in zip(own, beside)]
+        rim_low = jnp.where(upper, rim_beside, rim)
+        rim_high = jnp.where(upper, rim, rim_beside)
+        for tile, here in ((odd, low), (1 - odd, high)):
+            for x in range(TX):
+                cells = pl.ds(x * LANES, LANES)
+                now = here[x]
+                if here is low:
+                    before = pltpu.roll(rim_low, (LANES - width - width * x) % LANES, 1)
+                    after = high[x]
+                else:
+                    before = low[x]
+                    after = pltpu.roll(rim_high, (LANES - width * x) % LANES, 1)
+                at = [here[x + o] if 0 <= x + o < TX else zero for o in (1, -1, 2, -2)]
+                grad_ref[tile, 0, d, :, cells] = central(*at)
+                grad_ref[tile, 1, d, :, cells] = central(
+                    jnp.where(lane >= LANES - TZ, ahead(after, TZ), ahead(now, TZ)),
+                    jnp.where(lane < TZ, back(before, TZ), back(now, TZ)),
+                    jnp.where(lane >= LANES - width, ahead(after, width), ahead(now, width)),
+                    jnp.where(lane < width, back(before, width), back(now, width)),
+                )
+                grad_ref[tile, 2, d, :, cells] = central(
+                    jnp.where(in_z < TZ - 1, ahead(now, 1), 0.0),
+                    jnp.where(in_z >= 1, back(now, 1), 0.0),
+                    jnp.where(in_z < TZ - 2, ahead(now, 2), 0.0),
+                    jnp.where(in_z >= 2, back(now, 2), 0.0),
+                )
+
+
+def split(value):
+    high = value.astype(BF16)
+    return high, (value - high.astype(F32)).astype(BF16)
+
+
+def assemble_kernel(steps, *refs):
+    own, beside, weights, weights_beside = refs[:4]
+    first, second = refs[4 : 4 + steps], refs[4 + steps : 4 + 2 * steps]
+    first_swapped, second_swapped = refs[4 + 2 * steps : 4 + 3 * steps], refs[4 + 3 * steps : 4 + 4 * steps]
+    right_ref, left_ref, fields = refs[4 + 4 * steps :]
+    odd = lax.axis_index("space") % 2
+    place = lax.axis_index("mode")
+    block = own.shape[0] // 3
+    k_count = block // TX
+    blocks = steps + 1
+    modes = k_count * blocks
+
+    def put(tile, index, source):
+        for d in range(3):
+            begin = pl.multiple_of(d * modes * TX + index * block, block)
+            fields[tile, pl.ds(begin, block), :] = source[pl.ds(d * block, block), :]
+
+    put(0, place, own)
+    put(1, place, beside)
+    for hop in range(1, blocks):
+        below, above = place - hop, place + hop
+        for tile, direct, swapped in ((0, first, second_swapped), (1, second, first_swapped)):
+            for from_core, source in ((0, direct), (1, swapped)):
+                @pl.when((odd == from_core) & (below >= 0))
+                def _(tile=tile, source=source, below=below, hop=hop):
+                    put(tile, below, source[hop - 1])
+
+                @pl.when((odd != from_core) & (above < blocks))
+                def _(tile=tile, source=source, above=above, hop=hop):
+                    put(tile, above, source[hop - 1])
+
+    chips, shares = left_ref.shape[2:4]
+    for tile, weight in ((0, weights), (1, weights_beside)):
+        for d in range(3):
+            for x in range(TX):
+                cells = pl.ds(x * LANES, LANES)
+                chunk = fields[tile, pl.ds(d * modes * TX + x, modes, stride=TX), :]
+                high, low = split(chunk.T)
+                right_ref[tile, d, cells, pl.ds(0, modes)] = high
+                right_ref[tile, d, cells, pl.ds(modes, modes)] = low
+                for q in range(chips):
+                    begin = (d * modes + (2 * q + odd) * shares) * TX + x
+                    rows = fields[tile, pl.ds(begin, shares, stride=TX), :]
+                    left_ref[tile, d, q, :, cells] = rows * weight[pl.ds(x, 1), :]
+
+
+def tensor_kernel(apart, left_ref, grad_ref, right_ref, out_ref, total):
+    k_count = grad_ref.shape[3]
+    shares = out_ref.shape[0] // k_count
+    modes = out_ref.shape[1]
+    chip = lax.axis_index("space") // 2
+    target = chip ^ apart
+    total[...] = jnp.zeros_like(total)
+
+    def term(step, carry):
+        tile, e = step // 3, lax.rem(step, 3)
+        right = right_ref[tile, e]
+        highs, lows = [], []
+        for i in range(shares):
+            high_row, low_row = [], []
+            for x in range(TX):
+                cells = pl.ds(x * LANES, LANES)
+                value = None
+                for d in range(3):
+                    field = left_ref[tile, d, target, pl.ds(i, 1), cells]
+                    product = field * grad_ref[tile, e, d, :, cells]
+                    value = product if value is None else value + product
+                high, low = split(value)
+                high_row.append(high)
+                low_row.append(low)
+            highs.append(jnp.concatenate(high_row, 1))
+            lows.append(jnp.concatenate(low_row, 1))
+        total[...] += jnp.dot(
+            jnp.concatenate(highs, 0), right, preferred_element_type=F32
+        ) + jnp.dot(jnp.concatenate(lows, 0), right, preferred_element_type=F32)
+        return carry
+
+    lax.fori_loop(0, 6, term, 0)
+    out_ref[...] = total[:, :modes] + total[:, modes:]
+
+
+def per_device_paired(mode_fields, volume, fluid_mask):
+    k_count = mode_fields.shape[1]
+    places, tiles = lax.axis_size("mode"), lax.axis_size("space")
+    modes = k_count * places
+    shares = modes // tiles
+    own = mode_fields.reshape(3 * k_count * TX, LANES)
+    weights = (volume * fluid_mask.astype(F32)).reshape(TX, LANES)
+
+    def swap(value):
+        return lax.ppermute(value, "space", [(s, s ^ 1) for s in range(tiles)])
+
+    def hop(value, step):
+        pairs = []
+        for s in range(tiles):
+            for place in range(step - 1, places - 1):
+                if s % 2 == 0:
+                    pairs.append((s * places + place, s * places + place + 1))
+                else:
+                    mirrored = places - 1 - place
+                    pairs.append((s * places + mirrored, s * places + mirrored - 1))
+        return lax.ppermute(value, ("space", "mode"), pairs)
+
+    beside, weights_beside = swap(own), swap(weights)
+    rim = on_chip(rim_kernel, jax.ShapeDtypeStruct((3 * k_count, LANES), F32))(own)
+    beyond = [(s, s + 1) for s in range(1, tiles - 1, 2)]
+    rim = lax.ppermute(rim, "space", beyond + [(b, a) for a, b in beyond])
+    rim_beside = swap(rim)
+
+    first, second = [], []
+    for step in range(1, places):
+        first.append(hop(first[-1] if first else own, step))
+        second.append(hop(second[-1] if second else beside, step))
+    first_swapped = [swap(value) for value in first]
+    second_swapped = [swap(value) for value in second]
+
+    gradient = on_chip(
+        gradient_kernel, jax.ShapeDtypeStruct((2, 3, 3, k_count, CELLS), F32), flops=30_000_000
+    )(own, beside, rim, rim_beside)
+    right, left = on_chip(
+        functools.partial(assemble_kernel, places - 1),
+        [
+            jax.ShapeDtypeStruct((2, 3, CELLS, 2 * modes), BF16),
+            jax.ShapeDtypeStruct((2, 3, tiles // 2, shares, CELLS), F32),
+        ],
+        scratch=[pltpu.VMEM((2, 3 * modes * TX, LANES), F32)],
+    )(own, beside, weights, weights_beside, *first, *second, *first_swapped, *second_swapped)
+
+    def term(apart):
+        return on_chip(
+            functools.partial(tensor_kernel, apart),
+            jax.ShapeDtypeStruct((shares * k_count, modes), F32),
+            scratch=[pltpu.VMEM((shares * k_count, 2 * modes), F32)],
+            flops=4 * 2 * shares * k_count * modes * 6 * CELLS,
+        )(left, gradient, right)
+
+    received = []
+    for apart in range(tiles // 2 - 1, 0, -1):
+        pairs = [(s, s ^ (2 * apart)) for s in range(tiles)]
+        received.append(lax.ppermute(term(apart), "space", pairs))
+    total = term(0)
+    for value in received:
+        total = total + value
+    return total.reshape(shares, k_count, modes).transpose(0, 2, 1)
+
+
 def solution(mesh):
     in_specs = (P(None, "mode", "space", None), P("space", None), P("space", None))
     out_specs = P("space", None, "mode")
+    one_row = mesh.shape["space"] == TGY
     return jax.shard_map(
-        per_device, mesh=mesh, in_specs=in_specs, out_specs=out_specs, check_vma=False
+        per_device_paired if one_row else per_device_general,
+        mesh=mesh,
+        in_specs=in_specs,
+        out_specs=out_specs,
+        check_vma=False,
     )

time: 287 us -> 59.3 us (0.21); the launches traced: 282 us -> 59 us
  matrix products: 180 us -> 0 us
  waiting for transfers between devices: 41.7 us -> 12.3 us
  starting transfers between devices: 7.52 us -> 29.7 us
  blocking collectives: 21.2 us -> 0 us
  Pallas kernels: 0 us -> 14.5 us
  local copies, waits for them, and re-layouts: 14.7 us -> 0.92 us
  between operations: 13.9 us -> 0.2 us
    dot_general x4 -> x0, matrix products: 180 us -> none  [the longest x2 92.7 us: per_device(): jnp.einsum('dic,djkc->ijk', weighted, advected, precision=lax.Precision.H...]
    reduce_scatter x1 -> x0, waiting for transfers between devices: 41.6 us -> none  [per_device(): lax.psum_scatter(partial_tensor, 'space', scatter_dimension=0, tiled=True)]
    ppermute x4 -> x19, starting transfers between devices: 7.51 us -> 29.7 us  [the longest x9 14.3 us: swap(): return lax.ppermute(value, 'space', [(s, s ^ 1) for s in range(tiles)])]
    all_gather x1 -> x0, blocking collectives: 21.2 us -> none  [per_device(): everything = lax.all_gather(own_fields, 'mode', axis=1, tiled=True)]
    pallas_call x0 -> x7, Pallas kernels: none -> 14.5 us  [call(): pl.pallas_call(kernel, out_shape=out_shape, in_specs=[pl.BlockSpec(memory...]
    ppermute x4 -> x19, waiting for transfers between devices: 0.01 us -> 12.3 us  [the longest x3 8.98 us: per_device_paired(): received.append(lax.ppermute(term(apart), 'space', pairs))]
    reshape x8 -> x0, local copies, waits for them, and re-layouts: 4.85 us -> none  [the longest x2 1.16 us: per_device(): below_x = neighbour(upper_x, TGY).reshape(3, k_count, 2, TY, TZ)]
  transfers between devices with their start and end apart: 5 -> 19, of which waited for: 1 -> 5; matrix products, arithmetic and copies ran while one was open for 3% -> 1% of each run, Pallas kernels for 0% -> 9%
where the time goes in v1:
time: 59.3 us; the launch traced here: 59 us
  starting transfers between devices  29.7 us (50%)
  Pallas kernels  14.5 us (24%)
  waiting for transfers between devices  12.3 us (21%)
  other arithmetic  1.46 us (2%)
  local copies, waits for them, and re-layouts  0.92 us (2%)
    pallas_call x7, Pallas kernels, call(): pl.pallas_call(kernel, out_shape=out_shape, in_specs=[pl.BlockSpec(memory...  14.5 us
    ppermute x9, starting transfers between devices, swap(): return lax.ppermute(value, 'space', [(s, s ^ 1) for s in range(tiles)])  14.3 us
    ppermute x6, starting transfers between devices, hop(): return lax.ppermute(value, ('space', 'mode'), pairs)  10.6 us
    ppermute x3, waiting for transfers between devices, per_device_paired(): received.append(lax.ppermute(term(apart), 'space', pairs))  8.98 us
    ppermute x3, starting transfers between devices, per_device_paired(): received.append(lax.ppermute(term(apart), 'space', pairs))  4.09 us
    ppermute x6, waiting for transfers between devices, hop(): return lax.ppermute(value, ('space', 'mode'), pairs)  2.48 us
  transfers between devices with their start and end apart: 19, of which 5 were waited for; matrix products, arithmetic and copies ran while one was open for 1% of the time, Pallas kernels for 9%

profile of v1, /device:TPU:0, one launch (start us, length us, event | category | flops | bytes accessed | tf_op | source)
XLA Modules:
  0.0 59.0 jit_solution(7427137671551655977)
XLA Ops:
  0.0 0.5 collective-permute-start
  0.5 4.5 %collective-permute-start.2 = (f32[384,128]{1,0:T(8,128)}, f32[384,128]{1,0:T(8,128)S(1)}, u32[]{:S(2)}, u32[]{:S(2)}) collective-permute-start(f32[384,128]{1,0:T(8,128)} %bitcast.6), channel_id=1, source_target_pairs={{0,1},{1,2},{2,3},{7,6},{6,5},{5,4},{8,9},{9,10},{10,11},{15,14},{... | collective-permute-start | bytes 589832 | tf_op jit(solution)/shard_map/ppermute | solution.py:282
  4.9 0.0 collective-permute-done.refs_1_.beside_ref
  4.9 3.5 %collective-permute-start.5 = (f32[384,128]{1,0:T(8,128)S(1)}, f32[384,128]{1,0:T(8,128)S(1)}, u32[]{:S(2)}, u32[]{:S(2)}) collective-permute-start(f32[384,128]{1,0:T(8,128)S(1)} %collective-permute-done.refs_1_.beside_ref), channel_id=1, source_target_pairs={{0,1},{1,2},{2,3},{7,6},{6,5},{5,4},{8,9},{9,10},{10,11},{15,14},{... | collective-permute-start | bytes 589832 | tf_op jit(solution)/shard_map/ppermute | solution.py:282
  8.4 0.0 collective-permute-done.2.refs_4_
  8.5 0.7 %collective-permute-start.3 = (f32[384,128]{1,0:T(8,128)S(1)}, f32[384,128]{1,0:T(8,128)S(1)}, u32[]{:S(2)}, u32[]{:S(2)}) collective-permute-start(f32[384,128]{1,0:T(8,128)S(1)} %collective-permute-done.2.refs_4_), channel_id=1, source_target_pairs={{1,2},{2,3},{6,5},{5,4},{9,10},{10,11},{14,13},{13,12},{17,18},{18... | collective-permute-start | bytes 589832 | tf_op jit(solution)/shard_map/ppermute | solution.py:282
  9.1 2.5 %collective-permute-done.5.refs_7_ = f32[384,128]{1,0:T(8,128)S(1)} collective-permute-done((f32[384,128]{1,0:T(8,128)S(1)}, f32[384,128]{1,0:T(8,128)S(1)}, u32[]{:S(2)}, u32[]{:S(2)}) %collective-permute-start.5) | collective-permute-done | bytes 196640 | tf_op jit(solution)/shard_map/ppermute | solution.py:282
  11.6 0.7 %collective-permute-start.6 = (f32[384,128]{1,0:T(8,128)S(1)}, f32[384,128]{1,0:T(8,128)S(1)}, u32[]{:S(2)}, u32[]{:S(2)}) collective-permute-start(f32[384,128]{1,0:T(8,128)S(1)} %collective-permute-done.5.refs_7_), channel_id=1, source_target_pairs={{1,2},{2,3},{6,5},{5,4},{9,10},{10,11},{14,13},{13,12},{17,18},{18... | collective-permute-start | bytes 589832 | tf_op jit(solution)/shard_map/ppermute | solution.py:282
  12.3 0.9 %copy-done = f32[3,32,1,512]{3,2,1,0:T(1,128)S(1)} copy-done((f32[3,32,1,512]{3,2,1,0:T(1,128)S(1)}, f32[3,32,1,512]{3,2,1,0:T(1,128)}, u32[]{:S(2)}) %copy-start) | copy-done | bytes 196632
  13.2 0.2 shard_map.38
  13.4 0.7 %collective-permute-start.14 = (f32[96,128]{1,0:T(8,128)S(1)}, f32[96,128]{1,0:T(8,128)S(1)}, u32[]{:S(2)}, u32[]{:S(2)}) collective-permute-start(f32[96,128]{1,0:T(8,128)S(1)} %shard_map.38), channel_id=1, source_target_pairs={{4,8},{12,16},{20,24},{8,4},{16,12},{24,20},{5,9},{13,17},{21,25},... | collective-permute-start | bytes 147464 | tf_op jit(solution)/shard_map/ppermute | solution.py:287
  14.0 0.0 collective-permute-done.14.rim_ref
  14.0 4.6 %collective-permute-start.15 = (f32[96,128]{1,0:T(8,128)S(1)}, f32[96,128]{1,0:T(8,128)S(1)}, u32[]{:S(2)}, u32[]{:S(2)}) collective-permute-start(f32[96,128]{1,0:T(8,128)S(1)} %collective-permute-done.14.rim_ref), channel_id=1, source_target_pairs={{0,4},{4,0},{8,12},{12,8},{16,20},{20,16},{24,28},{28,24},{1,5},{5... | collective-permute-start | bytes 147464 | tf_op jit(solution)/shard_map/ppermute | solution.py:271
  18.6 0.0 collective-permute-start.8
  18.6 0.0 collective-permute-done.3.refs_5_
  18.6 0.7 %collective-permute-start.4 = (f32[384,128]{1,0:T(8,128)S(1)}, f32[384,128]{1,0:T(8,128)S(1)}, u32[]{:S(2)}, u32[]{:S(2)}) collective-permute-start(f32[384,128]{1,0:T(8,128)S(1)} %collective-permute-done.3.refs_5_), channel_id=1, source_target_pairs={{2,3},{5,4},{10,11},{13,12},{18,19},{21,20},{26,27},{29,28}} | collective-permute-start | bytes 589832 | tf_op jit(solution)/shard_map/ppermute | solution.py:282
  19.3 0.0 collective-permute-done.6.refs_8_
  19.3 0.7 %collective-permute-start.7 = (f32[384,128]{1,0:T(8,128)S(1)}, f32[384,128]{1,0:T(8,128)S(1)}, u32[]{:S(2)}, u32[]{:S(2)}) collective-permute-start(f32[384,128]{1,0:T(8,128)S(1)} %collective-permute-done.6.refs_8_), channel_id=1, source_target_pairs={{2,3},{5,4},{10,11},{13,12},{18,19},{21,20},{26,27},{29,28}} | collective-permute-start | bytes 589832 | tf_op jit(solution)/shard_map/ppermute | solution.py:282
  20.0 0.7 %convert_multiply_fusion = f32[1,512]{1,0:T(1,128)S(1)} fusion(f32[1,512]{1,0:T(1,128)} %param.4, s32[1,512]{1,0:T(1,128)} %param.5), kind=kLoop, calls=%fused_computation.1 | loop fusion | flops 1024 | bytes 6144 | tf_op jit(solution)/shard_map/mul | solution.py:268
  20.7 1.7 %collective-permute-start.1 = (f32[4,128]{1,0:T(4,128)S(1)}, f32[4,128]{1,0:T(4,128)S(1)}, u32[]{:S(2)}, u32[]{:S(2)}) collective-permute-start(f32[4,128]{1,0:T(4,128)S(1)} %bitcast.10), channel_id=1, source_target_pairs={{0,4},{4,0},{8,12},{12,8},{16,20},{20,16},{24,28},{28,24},{1,5},{5... | collective-permute-start | bytes 6152 | tf_op jit(solution)/shard_map/ppermute | solution.py:271
  22.5 0.8 %collective-permute-done.1.refs_3_ = f32[4,128]{1,0:T(4,128)S(1)} collective-permute-done((f32[4,128]{1,0:T(4,128)S(1)}, f32[4,128]{1,0:T(4,128)S(1)}, u32[]{:S(2)}, u32[]{:S(2)}) %collective-permute-start.1) | collective-permute-done | bytes 2080 | tf_op jit(solution)/shard_map/ppermute | solution.py:271
  23.3 0.3 collective-permute-start.11
  23.6 0.0 collective-permute-done.15.rim_beside_ref
  23.6 0.2 collective-permute-start.9
  23.8 0.0 collective-permute-done.8.refs_10_
  23.8 0.3 collective-permute-start.12
  24.1 0.0 collective-permute-done.4.refs_6_
  24.1 4.6 %collective-permute-start.10 = (f32[384,128]{1,0:T(8,128)S(1)}, f32[384,128]{1,0:T(8,128)S(1)}, u32[]{:S(2)}, u32[]{:S(2)}) collective-permute-start(f32[384,128]{1,0:T(8,128)S(1)} %collective-permute-done.4.refs_6_), channel_id=1, source_target_pairs={{0,4},{4,0},{8,12},{12,8},{16,20},{20,16},{24,28},{28,24},{1,5},{5... | collective-permute-start | bytes 589832 | tf_op jit(solution)/shard_map/ppermute | solution.py:271
  28.7 0.0 collective-permute-done.7.refs_9_
  28.7 2.1 %collective-permute-start.13 = (f32[384,128]{1,0:T(8,128)S(1)}, f32[384,128]{1,0:T(8,128)S(1)}, u32[]{:S(2)}, u32[]{:S(2)}) collective-permute-start(f32[384,128]{1,0:T(8,128)S(1)} %collective-permute-done.7.refs_9_), channel_id=1, source_target_pairs={{0,4},{4,0},{8,12},{12,8},{16,20},{20,16},{24,28},{28,24},{1,5},{5... | collective-permute-start | bytes 589832 | tf_op jit(solution)/shard_map/ppermute | solution.py:271
  30.8 2.2 %shard_map.39.grad_ref = f32[2,3,3,32,512]{4,3,2,1,0:T(8,128)S(1)} custom-call(f32[384,128]{1,0:T(8,128)S(1)} %bitcast.8, f32[384,128]{1,0:T(8,128)S(1)} %collective-permute-done.refs_1_.beside_ref, f32[96,128]{1,0:T(8,128)S(1)} %collective-permute-done.14.rim_ref, f32[96,128]{1,0:T(8,128)S(1)} %collective-permute-done.15.rim_beside_ref), custom_call_target="tpu_custom_call" | custom-call | flops 30000000 | bytes 1671168 | tf_op jit(solution)/shard_map/pallas_call | solution.py:90
  33.0 0.0 collective-permute-done.11.refs_13_
  33.0 0.0 collective-permute-done.9.refs_11_
  33.0 0.0 collective-permute-done.12.refs_14_
  33.0 0.0 collective-permute-done.10.refs_12_
  33.0 0.0 collective-permute-done.13.refs_15_
  33.1 0.7 %shard_map.37 = (bf16[2,3,512,256]{3,2,1,0:T(8,128)(2,1)S(1)}, f32[2,3,4,16,512]{4,3,2,1,0:T(8,128)S(1)}) custom-call(f32[384,128]{1,0:T(8,128)S(1)} %bitcast.9, f32[384,128]{1,0:T(8,128)S(1)} %collective-permute-done.refs_1_.beside_ref, f32[4,128]{1,0:T(4,128)S(1)} %bitcast.11, f32[4,128]{1,0:T(4,128)S(1)} %collective-permute-done.1.refs_3_, ...), custom_call_target="tpu_custom_call" | custom-call | bytes 5115904 | tf_op jit(solution)/shard_map/pallas_call | solution.py:90
  33.8 2.9 %shard_map.41 = f32[512,128]{1,0:T(8,128)S(1)} custom-call(f32[2,3,4,16,512]{4,3,2,1,0:T(8,128)S(1)} %get-tuple-element.7.left_ref, f32[2,3,3,32,512]{4,3,2,1,0:T(8,128)S(1)} %shard_map.39.grad_ref, bf16[2,3,512,256]{3,2,1,0:T(8,128)(2,1)S(1)} %get-tuple-element.8.right_ref), custom_call_target="tpu_custom_call" | custom-call | flops 1610612736 | bytes 3801088 | tf_op jit(solution)/shard_map/pallas_call | solution.py:90
  36.6 2.9 %shard_map.42 = f32[512,128]{1,0:T(8,128)S(1)} custom-call(f32[2,3,4,16,512]{4,3,2,1,0:T(8,128)S(1)} %get-tuple-element.7.left_ref, f32[2,3,3,32,512]{4,3,2,1,0:T(8,128)S(1)} %shard_map.39.grad_ref, bf16[2,3,512,256]{3,2,1,0:T(8,128)(2,1)S(1)} %get-tuple-element.8.right_ref), custom_call_target="tpu_custom_call" | custom-call | flops 1610612736 | bytes 3801088 | tf_op jit(solution)/shard_map/pallas_call | solution.py:90
  39.5 2.9 %shard_map.43 = f32[512,128]{1,0:T(8,128)S(1)} custom-call(f32[2,3,4,16,512]{4,3,2,1,0:T(8,128)S(1)} %get-tuple-element.7.left_ref, f32[2,3,3,32,512]{4,3,2,1,0:T(8,128)S(1)} %shard_map.39.grad_ref, bf16[2,3,512,256]{3,2,1,0:T(8,128)(2,1)S(1)} %get-tuple-element.8.right_ref), custom_call_target="tpu_custom_call" | custom-call | flops 1610612736 | bytes 3801088 | tf_op jit(solution)/shard_map/pallas_call | solution.py:90
  42.4 2.6 %collective-permute-start.16 = (f32[512,128]{1,0:T(8,128)S(1)}, f32[512,128]{1,0:T(8,128)S(1)}, u32[]{:S(2)}, u32[]{:S(2)}) collective-permute-start(f32[512,128]{1,0:T(8,128)S(1)} %shard_map.41), channel_id=1, source_target_pairs={{0,24},{4,28},{8,16},{12,20},{16,8},{20,12},{24,0},{28,4},{1,25},{... | collective-permute-start | bytes 786440 | tf_op jit(solution)/shard_map/ppermute | solution.py:320
  45.0 0.5 collective-permute-start.17
  45.5 1.0 %collective-permute-start.18 = (f32[512,128]{1,0:T(8,128)S(1)}, f32[512,128]{1,0:T(8,128)S(1)}, u32[]{:S(2)}, u32[]{:S(2)}) collective-permute-start(f32[512,128]{1,0:T(8,128)S(1)} %shard_map.43), channel_id=1, source_target_pairs={{0,8},{4,12},{8,0},{12,4},{16,24},{20,28},{24,16},{28,20},{1,9},{5... | collective-permute-start | bytes 786440 | tf_op jit(solution)/shard_map/ppermute | solution.py:320
  46.5 2.8 %shard_map.40 = f32[512,128]{1,0:T(8,128)S(1)} custom-call(f32[2,3,4,16,512]{4,3,2,1,0:T(8,128)S(1)} %get-tuple-element.7.left_ref, f32[2,3,3,32,512]{4,3,2,1,0:T(8,128)S(1)} %shard_map.39.grad_ref, bf16[2,3,512,256]{3,2,1,0:T(8,128)(2,1)S(1)} %get-tuple-element.8.right_ref), custom_call_target="tpu_custom_call" | custom-call | flops 1610612736 | bytes 3801088 | tf_op jit(solution)/shard_map/pallas_call | solution.py:90
  49.3 3.3 %collective-permute-done.16 = f32[512,128]{1,0:T(8,128)S(1)} collective-permute-done((f32[512,128]{1,0:T(8,128)S(1)}, f32[512,128]{1,0:T(8,128)S(1)}, u32[]{:S(2)}, u32[]{:S(2)}) %collective-permute-start.16) | collective-permute-done | bytes 262176 | tf_op jit(solution)/shard_map/ppermute | solution.py:320
  52.6 4.6 %collective-permute-done.17 = f32[512,128]{1,0:T(8,128)S(1)} collective-permute-done((f32[512,128]{1,0:T(8,128)S(1)}, f32[512,128]{1,0:T(8,128)S(1)}, u32[]{:S(2)}, u32[]{:S(2)}) %collective-permute-start.17) | collective-permute-done | bytes 262176 | tf_op jit(solution)/shard_map/ppermute | solution.py:320
  57.2 1.1 %collective-permute-done.18 = f32[512,128]{1,0:T(8,128)S(1)} collective-permute-done((f32[512,128]{1,0:T(8,128)S(1)}, f32[512,128]{1,0:T(8,128)S(1)}, u32[]{:S(2)}, u32[]{:S(2)}) %collective-permute-start.18) | collective-permute-done | bytes 262176 | tf_op jit(solution)/shard_map/ppermute | solution.py:320
  58.3 0.8 %add_add_fusion = f32[512,128]{1,0:T(8,128)} fusion(f32[512,128]{1,0:T(8,128)S(1)} %collective-permute-done.18, f32[512,128]{1,0:T(8,128)S(1)} %collective-permute-done.17, f32[512,128]{1,0:T(8,128)S(1)} %shard_map.40, f32[512,128]{1,0:T(8,128)S(1)} %collective-permute-done.16), kind=kLoop, calls=%fused_computation | loop fusion | flops 196608 | bytes 1310720 | tf_op jit(solution)/shard_map/add | solution.py:323
  (1 shorter events, 0.0 us)
Async XLA Ops:
  0.0 4.9 %collective-permute-start = (f32[384,128]{1,0:T(8,128)}, f32[384,128]{1,0:T(8,128)S(1)}, u32[]{:S(2)}, u32[]{:S(2)}) collective-permute-start(f32[384,128]{1,0:T(8,128)} %bitcast.5), channel_id=1, source_target_pairs={{0,4},{4,0},{8,12},{12,8},{16,20},{20,16},{24,28},{28,24},{1,5},{5... | collective-permute-start | bytes 589832 | tf_op jit(solution)/shard_map/ppermute | solution.py:271
  0.5 8.0 %collective-permute-start.2 = (f32[384,128]{1,0:T(8,128)}, f32[384,128]{1,0:T(8,128)S(1)}, u32[]{:S(2)}, u32[]{:S(2)}) collective-permute-start(f32[384,128]{1,0:T(8,128)} %bitcast.6), channel_id=1, source_target_pairs={{0,1},{1,2},{2,3},{7,6},{6,5},{5,4},{8,9},{9,10},{10,11},{15,14},{... | collective-permute-start | bytes 589832 | tf_op jit(solution)/shard_map/ppermute | solution.py:282
  4.9 6.7 %collective-permute-start.5 = (f32[384,128]{1,0:T(8,128)S(1)}, f32[384,128]{1,0:T(8,128)S(1)}, u32[]{:S(2)}, u32[]{:S(2)}) collective-permute-start(f32[384,128]{1,0:T(8,128)S(1)} %collective-permute-done.refs_1_.beside_ref), channel_id=1, source_target_pairs={{0,1},{1,2},{2,3},{7,6},{6,5},{5,4},{8,9},{9,10},{10,11},{15,14},{... | collective-permute-start | bytes 589832 | tf_op jit(solution)/shard_map/ppermute | solution.py:282
  8.5 10.2 %collective-permute-start.3 = (f32[384,128]{1,0:T(8,128)S(1)}, f32[384,128]{1,0:T(8,128)S(1)}, u32[]{:S(2)}, u32[]{:S(2)}) collective-permute-start(f32[384,128]{1,0:T(8,128)S(1)} %collective-permute-done.2.refs_4_), channel_id=1, source_target_pairs={{1,2},{2,3},{6,5},{5,4},{9,10},{10,11},{14,13},{13,12},{17,18},{18... | collective-permute-start | bytes 589832 | tf_op jit(solution)/shard_map/ppermute | solution.py:282
  11.6 7.7 %collective-permute-start.6 = (f32[384,128]{1,0:T(8,128)S(1)}, f32[384,128]{1,0:T(8,128)S(1)}, u32[]{:S(2)}, u32[]{:S(2)}) collective-permute-start(f32[384,128]{1,0:T(8,128)S(1)} %collective-permute-done.5.refs_7_), channel_id=1, source_target_pairs={{1,2},{2,3},{6,5},{5,4},{9,10},{10,11},{14,13},{13,12},{17,18},{18... | collective-permute-start | bytes 589832 | tf_op jit(solution)/shard_map/ppermute | solution.py:282
  12.3 0.9 %copy-start = (f32[3,32,1,512]{3,2,1,0:T(1,128)S(1)}, f32[3,32,1,512]{3,2,1,0:T(1,128)}, u32[]{:S(2)}) copy-start(f32[3,32,1,512]{3,2,1,0:T(1,128)} %param.3) | copy-start | bytes 589828
  13.4 0.7 %collective-permute-start.14 = (f32[96,128]{1,0:T(8,128)S(1)}, f32[96,128]{1,0:T(8,128)S(1)}, u32[]{:S(2)}, u32[]{:S(2)}) collective-permute-start(f32[96,128]{1,0:T(8,128)S(1)} %shard_map.38), channel_id=1, source_target_pairs={{4,8},{12,16},{20,24},{8,4},{16,12},{24,20},{5,9},{13,17},{21,25},... | collective-permute-start | bytes 147464 | tf_op jit(solution)/shard_map/ppermute | solution.py:287
  14.0 9.6 %collective-permute-start.15 = (f32[96,128]{1,0:T(8,128)S(1)}, f32[96,128]{1,0:T(8,128)S(1)}, u32[]{:S(2)}, u32[]{:S(2)}) collective-permute-start(f32[96,128]{1,0:T(8,128)S(1)} %collective-permute-done.14.rim_ref), channel_id=1, source_target_pairs={{0,4},{4,0},{8,12},{12,8},{16,20},{20,16},{24,28},{28,24},{1,5},{5... | collective-permute-start | bytes 147464 | tf_op jit(solution)/shard_map/ppermute | solution.py:271
  18.6 5.2 %collective-permute-start.8 = (f32[384,128]{1,0:T(8,128)S(1)}, f32[384,128]{1,0:T(8,128)S(1)}, u32[]{:S(2)}, u32[]{:S(2)}) collective-permute-start(f32[384,128]{1,0:T(8,128)S(1)} %collective-permute-done.2.refs_4_), channel_id=1, source_target_pairs={{0,4},{4,0},{8,12},{12,8},{16,20},{20,16},{24,28},{28,24},{1,5},{5... | collective-permute-start | bytes 589832 | tf_op jit(solution)/shard_map/ppermute | solution.py:271
  18.6 5.5 %collective-permute-start.4 = (f32[384,128]{1,0:T(8,128)S(1)}, f32[384,128]{1,0:T(8,128)S(1)}, u32[]{:S(2)}, u32[]{:S(2)}) collective-permute-start(f32[384,128]{1,0:T(8,128)S(1)} %collective-permute-done.3.refs_5_), channel_id=1, source_target_pairs={{2,3},{5,4},{10,11},{13,12},{18,19},{21,20},{26,27},{29,28}} | collective-permute-start | bytes 589832 | tf_op jit(solution)/shard_map/ppermute | solution.py:282
  19.3 9.4 %collective-permute-start.7 = (f32[384,128]{1,0:T(8,128)S(1)}, f32[384,128]{1,0:T(8,128)S(1)}, u32[]{:S(2)}, u32[]{:S(2)}) collective-permute-start(f32[384,128]{1,0:T(8,128)S(1)} %collective-permute-done.6.refs_8_), channel_id=1, source_target_pairs={{2,3},{5,4},{10,11},{13,12},{18,19},{21,20},{26,27},{29,28}} | collective-permute-start | bytes 589832 | tf_op jit(solution)/shard_map/ppermute | solution.py:282
  20.7 2.6 %collective-permute-start.1 = (f32[4,128]{1,0:T(4,128)S(1)}, f32[4,128]{1,0:T(4,128)S(1)}, u32[]{:S(2)}, u32[]{:S(2)}) collective-permute-start(f32[4,128]{1,0:T(4,128)S(1)} %bitcast.10), channel_id=1, source_target_pairs={{0,4},{4,0},{8,12},{12,8},{16,20},{20,16},{24,28},{28,24},{1,5},{5... | collective-permute-start | bytes 6152 | tf_op jit(solution)/shard_map/ppermute | solution.py:271
  23.3 9.7 %collective-permute-start.11 = (f32[384,128]{1,0:T(8,128)S(1)}, f32[384,128]{1,0:T(8,128)S(1)}, u32[]{:S(2)}, u32[]{:S(2)}) collective-permute-start(f32[384,128]{1,0:T(8,128)S(1)} %collective-permute-done.5.refs_7_), channel_id=1, source_target_pairs={{0,4},{4,0},{8,12},{12,8},{16,20},{20,16},{24,28},{28,24},{1,5},{5... | collective-permute-start | bytes 589832 | tf_op jit(solution)/shard_map/ppermute | solution.py:271
  23.6 9.4 %collective-permute-start.9 = (f32[384,128]{1,0:T(8,128)S(1)}, f32[384,128]{1,0:T(8,128)S(1)}, u32[]{:S(2)}, u32[]{:S(2)}) collective-permute-start(f32[384,128]{1,0:T(8,128)S(1)} %collective-permute-done.3.refs_5_), channel_id=1, source_target_pairs={{0,4},{4,0},{8,12},{12,8},{16,20},{20,16},{24,28},{28,24},{1,5},{5... | collective-permute-start | bytes 589832 | tf_op jit(solution)/shard_map/ppermute | solution.py:271
  23.8 9.2 %collective-permute-start.12 = (f32[384,128]{1,0:T(8,128)S(1)}, f32[384,128]{1,0:T(8,128)S(1)}, u32[]{:S(2)}, u32[]{:S(2)}) collective-permute-start(f32[384,128]{1,0:T(8,128)S(1)} %collective-permute-done.6.refs_8_), channel_id=1, source_target_pairs={{0,4},{4,0},{8,12},{12,8},{16,20},{20,16},{24,28},{28,24},{1,5},{5... | collective-permute-start | bytes 589832 | tf_op jit(solution)/shard_map/ppermute | solution.py:271
  24.1 8.9 %collective-permute-start.10 = (f32[384,128]{1,0:T(8,128)S(1)}, f32[384,128]{1,0:T(8,128)S(1)}, u32[]{:S(2)}, u32[]{:S(2)}) collective-permute-start(f32[384,128]{1,0:T(8,128)S(1)} %collective-permute-done.4.refs_6_), channel_id=1, source_target_pairs={{0,4},{4,0},{8,12},{12,8},{16,20},{20,16},{24,28},{28,24},{1,5},{5... | collective-permute-start | bytes 589832 | tf_op jit(solution)/shard_map/ppermute | solution.py:271
  28.7 4.3 %collective-permute-start.13 = (f32[384,128]{1,0:T(8,128)S(1)}, f32[384,128]{1,0:T(8,128)S(1)}, u32[]{:S(2)}, u32[]{:S(2)}) collective-permute-start(f32[384,128]{1,0:T(8,128)S(1)} %collective-permute-done.7.refs_9_), channel_id=1, source_target_pairs={{0,4},{4,0},{8,12},{12,8},{16,20},{20,16},{24,28},{28,24},{1,5},{5... | collective-permute-start | bytes 589832 | tf_op jit(solution)/shard_map/ppermute | solution.py:271
  42.4 10.2 %collective-permute-start.16 = (f32[512,128]{1,0:T(8,128)S(1)}, f32[512,128]{1,0:T(8,128)S(1)}, u32[]{:S(2)}, u32[]{:S(2)}) collective-permute-start(f32[512,128]{1,0:T(8,128)S(1)} %shard_map.41), channel_id=1, source_target_pairs={{0,24},{4,28},{8,16},{12,20},{16,8},{20,12},{24,0},{28,4},{1,25},{... | collective-permute-start | bytes 786440 | tf_op jit(solution)/shard_map/ppermute | solution.py:320
  45.0 12.2 %collective-permute-start.17 = (f32[512,128]{1,0:T(8,128)S(1)}, f32[512,128]{1,0:T(8,128)S(1)}, u32[]{:S(2)}, u32[]{:S(2)}) collective-permute-start(f32[512,128]{1,0:T(8,128)S(1)} %shard_map.42), channel_id=1, source_target_pairs={{0,16},{4,20},{8,24},{12,28},{16,0},{20,4},{24,8},{28,12},{1,17},{... | collective-permute-start | bytes 786440 | tf_op jit(solution)/shard_map/ppermute | solution.py:320
  45.5 12.8 %collective-permute-start.18 = (f32[512,128]{1,0:T(8,128)S(1)}, f32[512,128]{1,0:T(8,128)S(1)}, u32[]{:S(2)}, u32[]{:S(2)}) collective-permute-start(f32[512,128]{1,0:T(8,128)S(1)} %shard_map.43), channel_id=1, source_target_pairs={{0,8},{4,12},{8,0},{12,4},{16,24},{20,28},{24,16},{28,20},{1,9},{5... | collective-permute-start | bytes 786440 | tf_op jit(solution)/shard_map/ppermute | solution.py:320

commit v2 on v0

--- a/solution.py
+++ b/solution.py
@@ -1,6 +1,10 @@
+import functools
+
 import jax
 import jax.numpy as jnp
 from jax import lax
+from jax.experimental import pallas as pl
+from jax.experimental.pallas import tpu as pltpu
 from jax.sharding import PartitionSpec as P
 
 M = 128
@@ -28,7 +32,7 @@
     return passed_along(rim_block, "space", offset)
 
 
-def per_device(mode_fields, volume, fluid_mask):
+def per_device_general(mode_fields, volume, fluid_mask):
     k_count = mode_fields.shape[1]
     cell_count = mode_fields.shape[3]
     rim_rows = 3 * k_count
@@ -71,9 +75,217 @@
     return lax.psum_scatter(partial_tensor, "space", scatter_dimension=0, tiled=True)
 
 
+LANES = TY * TZ
+CELLS = TX * LANES
+F32 = jnp.float32
+BF16 = jnp.bfloat16
+MIB = 1 << 20
+
+
+def on_chip(kernel, out_shape, scratch=(), in_place=0, limit=48):
+
+    def call(*operands):
+        return pl.pallas_call(
+            kernel,
+            out_shape=out_shape,
+            in_specs=[pl.BlockSpec(memory_space=pl.ANY)] * in_place
+            + [pl.BlockSpec(memory_space=pltpu.VMEM)] * (len(operands) - in_place),
+            out_specs=jax.tree.map(lambda _: pl.BlockSpec(memory_space=pltpu.VMEM), out_shape),
+            scratch_shapes=list(scratch),
+            compiler_params=pltpu.CompilerParams(vmem_limit_bytes=limit * MIB),
+            cost_estimate=pl.CostEstimate(flops=2_000_000_000, bytes_accessed=1_000_000, transcendentals=0),
+        )(*operands)
+
+    return call
+
+
+def lane_index(rows):
+    return lax.broadcasted_iota(jnp.int32, (rows, LANES), 1)
+
+
+def rim_kernel(own_ref, inner_ref, outer_ref):
+    rows = inner_ref.shape[0]
+    upper = lax.axis_index("space") % 2 == 1
+    lane = lane_index(rows)
+    width = 2 * TZ
+    firsts = jnp.zeros((rows, LANES), F32)
+    lasts = firsts
+    for x in range(TX):
+        chunk = own_ref[pl.ds(x, rows, stride=TX), :]
+        inside = (lane >= width * x) & (lane < width * (x + 1))
+        firsts = jnp.where(inside, pltpu.roll(chunk, (width * x) % LANES, 1), firsts)
+        lasts = jnp.where(inside, pltpu.roll(chunk, (width * x + width) % LANES, 1), lasts)
+    inner_ref[...] = jnp.where(upper, firsts, lasts)
+    outer_ref[...] = jnp.where(upper, lasts, firsts)
+
+
+def write_gradient(own_ref, inner_ref, outer_ref, grad_ref):
+    k_count = grad_ref.shape[2]
+    upper = lax.axis_index("space") % 2 == 1
+    lane = lane_index(k_count)
+    in_z = lane % TZ
+    width = 2 * TZ
+
+    def back(value, by):
+        return pltpu.roll(value, by, 1)
+
+    def ahead(value, by):
+        return pltpu.roll(value, LANES - by, 1)
+
+    def central(plus1, minus1, plus2, minus2):
+        return (plus1 - minus1) * (2.0 / 3.0) - (plus2 - minus2) * (1.0 / 12.0)
+
+    zero = jnp.zeros((k_count, LANES), F32)
+    for d in range(3):
+        rows = pl.ds(d * k_count, k_count)
+        inner, outer = inner_ref[rows, :], outer_ref[rows, :]
+        rim_before = jnp.where(upper, inner, outer)
+        rim_after = jnp.where(upper, outer, inner)
+        own = [own_ref[pl.ds(d * k_count * TX + x, k_count, stride=TX), :] for x in range(TX)]
+        for x in range(TX):
+            cells = pl.ds(x * LANES, LANES)
+            now = own[x]
+            before = pltpu.roll(rim_before, (LANES - width - width * x) % LANES, 1)
+            after = pltpu.roll(rim_after, (LANES - width * x) % LANES, 1)
+            at = [own[x + o] if 0 <= x + o < TX else zero for o in (1, -1, 2, -2)]
+            grad_ref[0, d, :, cells] = central(*at)
+            grad_ref[1, d, :, cells] = central(
+                jnp.where(lane >= LANES - TZ, ahead(after, TZ), ahead(now, TZ)),
+                jnp.where(lane < TZ, back(before, TZ), back(now, TZ)),
+                jnp.where(lane >= LANES - width, ahead(after, width), ahead(now, width)),
+                jnp.where(lane < width, back(before, width), back(now, width)),
+            )
+            grad_ref[2, d, :, cells] = central(
+                jnp.where(in_z < TZ - 1, ahead(now, 1), 0.0),
+                jnp.where(in_z >= 1, back(now, 1), 0.0),
+                jnp.where(in_z < TZ - 2, ahead(now, 2), 0.0),
+                jnp.where(in_z >= 2, back(now, 2), 0.0),
+            )
+
+
+def split(value):
+    high = value.astype(BF16)
+    return high, (value - high.astype(F32)).astype(BF16)
+
+
+def prepare_kernel(
+    fields_hbm, own_ref, inner_ref, outer_ref, volume_ref, mask_ref, grad_ref, right_ref, left_ref, fields_ref, arrived
+):
+    copy = pltpu.make_async_copy(fields_hbm, fields_ref, arrived)
+    copy.start()
+    write_gradient(own_ref, inner_ref, outer_ref, grad_ref)
+    copy.wait()
+    blocks, block = fields_ref.shape[:2]
+    k_count = block // (3 * TX)
+    modes = blocks * k_count
+    chips, cores, shares = left_ref.shape[1:4]
+    weights = volume_ref[...] * mask_ref[...].astype(F32)
+    for d in range(3):
+        for x in range(TX):
+            cells = pl.ds(x * LANES, LANES)
+            rows = pl.ds(d * k_count * TX + x, k_count, stride=TX)
+            chunk = jnp.concatenate([fields_ref[b, rows, :] for b in range(blocks)], 0)
+            high, low = split(chunk.T)
+            right_ref[d, cells, pl.ds(0, modes)] = high
+            right_ref[d, cells, pl.ds(modes, modes)] = low
+            weighted = chunk * weights[x : x + 1]
+            for q in range(chips):
+                for c in range(cores):
+                    begin = (q * cores + c) * shares
+                    left_ref[d, q, c, :, cells] = weighted[begin : begin + shares]
+
+
+def tensor_kernel(apart, other, left_ref, grad_ref, right_ref, *refs):
+    given, out_ref = refs[:-1], refs[-1]
+    k_count = grad_ref.shape[2]
+    shares = left_ref.shape[3]
+    modes = out_ref.shape[1]
+    place = lax.axis_index("space")
+    chip, core = (place // 2) ^ apart, (place % 2) ^ other
+    highs, lows = [], []
+    for i in range(shares):
+        high_row, low_row = [], []
+        for e in range(3):
+            for x in range(TX):
+                cells = pl.ds(x * LANES, LANES)
+                value = None
+                for d in range(3):
+                    field = left_ref[d, chip, core, pl.ds(i, 1), cells]
+                    product = field * grad_ref[e, d, :, cells]
+                    value = product if value is None else value + product
+                high, low = split(value)
+                high_row.append(high)
+                low_row.append(low)
+        highs.append(jnp.concatenate(high_row, 1))
+        lows.append(jnp.concatenate(low_row, 1))
+    right = right_ref[...].reshape(3 * CELLS, 2 * modes)
+    total = jnp.dot(
+        jnp.concatenate(highs, 0), right, preferred_element_type=F32
+    ) + jnp.dot(jnp.concatenate(lows, 0), right, preferred_element_type=F32)
+    total = total[:, :modes] + total[:, modes:]
+    for more in given:
+        total = total + more[...]
+    out_ref[...] = total
+
+
+def per_device_paired(mode_fields, volume, fluid_mask):
+    k_count = mode_fields.shape[1]
+    places, tiles = lax.axis_size("mode"), lax.axis_size("space")
+    modes = k_count * places
+    shares = modes // tiles
+    own = mode_fields.reshape(3 * k_count * TX, LANES)
+
+    def swap(value):
+        return lax.ppermute(value, "space", [(s, s ^ 1) for s in range(tiles)])
+
+    fields = lax.all_gather(own, "mode", axis=0, tiled=False)
+    inner, outer = on_chip(rim_kernel, [jax.ShapeDtypeStruct((3 * k_count, LANES), F32)] * 2)(own)
+    beyond = [(s, s + 1) for s in range(1, tiles - 1, 2)]
+    outer = lax.ppermute(outer, "space", beyond + [(b, a) for a, b in beyond])
+    inner = swap(inner)
+    fields, inner, outer = lax.optimization_barrier((fields, inner, outer))
+    gradient, right, left = on_chip(
+        prepare_kernel,
+        [
+            jax.ShapeDtypeStruct((3, 3, k_count, CELLS), F32),
+            jax.ShapeDtypeStruct((3, CELLS, 2 * modes), BF16),
+            jax.ShapeDtypeStruct((3, tiles // 2, 2, shares, CELLS), F32),
+        ],
+        scratch=[pltpu.VMEM(fields.shape, F32), pltpu.SemaphoreType.DMA],
+        in_place=1,
+    )(fields, own, inner, outer, volume.reshape(TX, LANES), fluid_mask.reshape(TX, LANES))
+
+    def term(apart, other, *given):
+        return on_chip(
+            functools.partial(tensor_kernel, apart, other),
+            jax.ShapeDtypeStruct((shares * k_count, modes), F32),
+        )(left, gradient, right, *given)
+
+    def send(apart, value):
+        return lax.ppermute(value, "space", [(s, s ^ (2 * apart)) for s in range(tiles)])
+
+    aparts = list(range(tiles // 2 - 1, -1, -1))
+    shared = {aparts[0]: swap(term(aparts[0], 1))}
+    received = []
+    for now, later in zip(aparts, aparts[1:]):
+        shared[later] = swap(term(later, 1))
+        value = term(now, 0, shared[now])
+        received.append(send(now, value))
+        left, value = lax.optimization_barrier((left, value))
+    total = term(0, 0, shared[0], received[0])
+    for value in received[1:]:
+        total = total + value
+    return total.reshape(shares, k_count, modes).transpose(0, 2, 1)
+
+
 def solution(mesh):
     in_specs = (P(None, "mode", "space", None), P("space", None), P("space", None))
     out_specs = P("space", None, "mode")
+    one_row = mesh.shape["space"] == TGY
     return jax.shard_map(
-        per_device, mesh=mesh, in_specs=in_specs, out_specs=out_specs, check_vma=False
+        per_device_paired if one_row else per_device_general,
+        mesh=mesh,
+        in_specs=in_specs,
+        out_specs=out_specs,
+        check_vma=False,
     )

time: 287 us -> 47.9 us (0.17); the launches traced: 282 us -> 47.7 us
  matrix products: 180 us -> 0 us
  waiting for transfers between devices: 41.7 us -> 6.32 us
  between operations: 13.9 us -> 0.12 us
  local copies, waits for them, and re-layouts: 14.7 us -> 1.6 us
  Pallas kernels: 0 us -> 9.84 us
    dot_general x4 -> x0, matrix products: 180 us -> none  [the longest x2 92.7 us: per_device(): jnp.einsum('dic,djkc->ijk', weighted, advected, precision=lax.Precision.H...]
    reduce_scatter x1 -> x0, waiting for transfers between devices: 41.6 us -> none  [per_device(): lax.psum_scatter(partial_tensor, 'space', scatter_dimension=0, tiled=True)]
    pallas_call x0 -> x10, Pallas kernels: none -> 9.84 us  [call(): pl.pallas_call(kernel, out_shape=out_shape, in_specs=[pl.BlockSpec(memory...]
    ppermute x4 -> x9, waiting for transfers between devices: 0.01 us -> 6.32 us  [the longest x3 6.22 us: send(): lax.ppermute(value, 'space', [(s, s ^ 2 * apart) for s in range(tiles)])]
    reshape x8 -> x0, local copies, waits for them, and re-layouts: 4.85 us -> none  [the longest x2 1.16 us: per_device(): below_x = neighbour(upper_x, TGY).reshape(3, k_count, 2, TY, TZ)]
    ppermute x4 -> x9, starting transfers between devices: 7.51 us -> 9.8 us  [the longest x3 6.25 us: send(): lax.ppermute(value, 'space', [(s, s ^ 2 * apart) for s in range(tiles)])]
  transfers between devices with their start and end apart: 5 -> 9, of which waited for: 1 -> 4; matrix products, arithmetic and copies ran while one was open for 3% -> 0% of each run, Pallas kernels for 0% -> 15%
where the time goes in v2:
time: 47.9 us; the launch traced here: 47.7 us
  blocking collectives  19.3 us (40%)
  Pallas kernels  9.84 us (21%)
  starting transfers between devices  9.8 us (20%)
  waiting for transfers between devices  6.32 us (13%)
  local copies, waits for them, and re-layouts  1.6 us (3%)
  other arithmetic  0.76 us (2%)
    all_gather x1, blocking collectives, per_device_paired(): fields = lax.all_gather(own, 'mode', axis=0, tiled=False)  19.3 us
    pallas_call x10, Pallas kernels, call(): pl.pallas_call(kernel, out_shape=out_shape, in_specs=[pl.BlockSpec(memory...  9.84 us
    ppermute x3, starting transfers between devices, send(): lax.ppermute(value, 'space', [(s, s ^ 2 * apart) for s in range(tiles)])  6.25 us
    ppermute x3, waiting for transfers between devices, send(): lax.ppermute(value, 'space', [(s, s ^ 2 * apart) for s in range(tiles)])  6.22 us
    ppermute x5, starting transfers between devices, swap(): return lax.ppermute(value, 'space', [(s, s ^ 1) for s in range(tiles)])  2.89 us
    unnamed x6, local copies, waits for them, and re-layouts  1.6 us
  transfers between devices with their start and end apart: 9, of which 4 were waited for; matrix products, arithmetic and copies ran while one was open for 0% of the time, Pallas kernels for 15%

profile of v2, /device:TPU:0, one launch (start us, length us, event | category | flops | bytes accessed | tf_op | source)
XLA Modules:
  0.0 47.7 jit_solution(10407478550574567609)
XLA Ops:
  0.0 0.0 copy-start
  0.0 0.9 %copy-done = f32[3,32,1,512]{3,2,1,0:T(1,128)S(1)} copy-done((f32[3,32,1,512]{3,2,1,0:T(1,128)S(1)}, f32[3,32,1,512]{3,2,1,0:T(1,128)}, u32[]{:S(2)}) %copy-start) | copy-done | bytes 196632
  0.9 0.2 shard_map.37
  1.1 0.5 %collective-permute-start = (f32[96,128]{1,0:T(8,128)S(1)}, f32[96,128]{1,0:T(8,128)S(1)}, u32[]{:S(2)}, u32[]{:S(2)}) collective-permute-start(f32[96,128]{1,0:T(8,128)S(1)} %get-tuple-element.16), channel_id=1, source_target_pairs={{0,4},{4,0},{8,12},{12,8},{16,20},{20,16},{24,28},{28,24},{1,5},{5... | collective-permute-start | bytes 147464 | tf_op jit(solution)/shard_map/ppermute | solution.py:239
  1.6 0.7 %collective-permute-start.1 = (f32[96,128]{1,0:T(8,128)S(1)}, f32[96,128]{1,0:T(8,128)S(1)}, u32[]{:S(2)}, u32[]{:S(2)}) collective-permute-start(f32[96,128]{1,0:T(8,128)S(1)} %get-tuple-element.17), channel_id=1, source_target_pairs={{4,8},{12,16},{20,24},{8,4},{16,12},{24,20},{5,9},{13,17},{21,25},... | collective-permute-start | bytes 147464 | tf_op jit(solution)/shard_map/ppermute | solution.py:244
  2.3 0.0 copy-start.2
  2.3 19.3 %all_gather.3.fields_hbm = f32[4,384,128]{2,1,0:T(8,128)S(1)} all-gather(f32[1,384,128]{2,1,0:T(8,128)S(1)} %bitcast.8), channel_id=1, replica_groups=mesh['space'=8,'mode'=4] {'mode'}, dimensions={0}, use_global_device_ids=true | all-gather | bytes 983040 | tf_op jit(solution)/shard_map/all_gather | solution.py:241
  21.6 0.0 copy-start.1
  21.6 0.0 collective-permute-done.inner_ref
  21.6 0.0 collective-permute-done.1.outer_ref
  21.6 0.0 copy-done.2
  21.6 0.7 %copy-done.1 = f32[1,512]{1,0:T(1,128)S(1)} copy-done((f32[1,512]{1,0:T(1,128)S(1)}, f32[1,512]{1,0:T(1,128)}, u32[]{:S(2)}) %copy-start.1) | copy-done | bytes 2072
  22.2 1.7 %shard_map.38 = (f32[3,3,32,512]{3,2,1,0:T(8,128)S(1)}, bf16[3,512,256]{2,1,0:T(8,128)(2,1)S(1)}, f32[3,4,2,16,512]{4,3,2,1,0:T(8,128)S(1)}) custom-call(f32[4,384,128]{2,1,0:T(8,128)S(1)} %all_gather.3.fields_hbm, f32[384,128]{1,0:T(8,128)S(1)} %bitcast.9, f32[96,128]{1,0:T(8,128)S(1)} %collective-permute-done.inner_ref, ...), custom_call_target="tpu_custom_call" | custom-call | flops 2000000000 | bytes 1000000 | tf_op jit(solution)/shard_map/pallas_call | solution.py:88
  24.0 1.0 %shard_map.39 = f32[512,128]{1,0:T(8,128)S(1)} custom-call(f32[3,4,2,16,512]{4,3,2,1,0:T(8,128)S(1)} %get-tuple-element.26.left_ref, f32[3,3,32,512]{3,2,1,0:T(8,128)S(1)} %get-tuple-element.22.grad_ref, bf16[3,512,256]{2,1,0:T(8,128)(2,1)S(1)} %get-tuple-element.23.right_ref), custom_call_target="tpu_custom_call" | custom-call | flops 2000000000 | bytes 1000000 | tf_op jit(solution)/shard_map/pallas_call | solution.py:88
  25.0 1.7 %collective-permute-start.2 = (f32[512,128]{1,0:T(8,128)S(1)}, f32[512,128]{1,0:T(8,128)S(1)}, u32[]{:S(2)}, u32[]{:S(2)}) collective-permute-start(f32[512,128]{1,0:T(8,128)S(1)} %shard_map.39), channel_id=1, source_target_pairs={{0,4},{4,0},{8,12},{12,8},{16,20},{20,16},{24,28},{28,24},{1,5},{5... | collective-permute-start | bytes 786440 | tf_op jit(solution)/shard_map/ppermute | solution.py:239
  26.7 1.0 %shard_map.41 = f32[512,128]{1,0:T(8,128)S(1)} custom-call(f32[3,4,2,16,512]{4,3,2,1,0:T(8,128)S(1)} %get-tuple-element.26.left_ref, f32[3,3,32,512]{3,2,1,0:T(8,128)S(1)} %get-tuple-element.22.grad_ref, bf16[3,512,256]{2,1,0:T(8,128)(2,1)S(1)} %get-tuple-element.23.right_ref), custom_call_target="tpu_custom_call" | custom-call | flops 2000000000 | bytes 1000000 | tf_op jit(solution)/shard_map/pallas_call | solution.py:88
  27.7 0.1 collective-permute-start.3
  27.7 0.1 collective-permute-done.2.refs_0_
  27.8 1.0 %shard_map.40 = f32[512,128]{1,0:T(8,128)S(1)} custom-call(f32[3,4,2,16,512]{4,3,2,1,0:T(8,128)S(1)} %get-tuple-element.26.left_ref, f32[3,3,32,512]{3,2,1,0:T(8,128)S(1)} %get-tuple-element.22.grad_ref, bf16[3,512,256]{2,1,0:T(8,128)(2,1)S(1)} %get-tuple-element.23.right_ref, f32[512,128]{1,0:T(8,128)S(1)} %collective-permute-done.2.refs_0_), custom_call_target="tpu_custom_call" | custom-call | flops 2000000000 | bytes 1000000 | tf_op jit(solution)/shard_map/pallas_call | solution.py:88
  28.8 4.6 %collective-permute-start.6 = (f32[512,128]{1,0:T(8,128)S(1)}, f32[512,128]{1,0:T(8,128)S(1)}, u32[]{:S(2)}, u32[]{:S(2)}) collective-permute-start(f32[512,128]{1,0:T(8,128)S(1)} %shard_map.40), channel_id=1, source_target_pairs={{0,24},{4,28},{8,16},{12,20},{16,8},{20,12},{24,0},{28,4},{1,25},{... | collective-permute-start | bytes 786440 | tf_op jit(solution)/shard_map/ppermute | solution.py:265
  33.4 1.0 %shard_map.43 = f32[512,128]{1,0:T(8,128)S(1)} custom-call(f32[3,4,2,16,512]{4,3,2,1,0:T(8,128)S(1)} %get-tuple-element.26.left_ref, f32[3,3,32,512]{3,2,1,0:T(8,128)S(1)} %get-tuple-element.22.grad_ref, bf16[3,512,256]{2,1,0:T(8,128)(2,1)S(1)} %get-tuple-element.23.right_ref), custom_call_target="tpu_custom_call" | custom-call | flops 2000000000 | bytes 1000000 | tf_op jit(solution)/shard_map/pallas_call | solution.py:88
  34.4 0.1 collective-permute-start.4
  34.5 0.0 collective-permute-done.3.refs_0_
  34.5 1.0 %shard_map.42 = f32[512,128]{1,0:T(8,128)S(1)} custom-call(f32[3,4,2,16,512]{4,3,2,1,0:T(8,128)S(1)} %get-tuple-element.26.left_ref, f32[3,3,32,512]{3,2,1,0:T(8,128)S(1)} %get-tuple-element.22.grad_ref, bf16[3,512,256]{2,1,0:T(8,128)(2,1)S(1)} %get-tuple-element.23.right_ref, f32[512,128]{1,0:T(8,128)S(1)} %collective-permute-done.3.refs_0_), custom_call_target="tpu_custom_call" | custom-call | flops 2000000000 | bytes 1000000 | tf_op jit(solution)/shard_map/pallas_call | solution.py:88
  35.5 1.0 %shard_map.45 = f32[512,128]{1,0:T(8,128)S(1)} custom-call(f32[3,4,2,16,512]{4,3,2,1,0:T(8,128)S(1)} %get-tuple-element.26.left_ref, f32[3,3,32,512]{3,2,1,0:T(8,128)S(1)} %get-tuple-element.22.grad_ref, bf16[3,512,256]{2,1,0:T(8,128)(2,1)S(1)} %get-tuple-element.23.right_ref), custom_call_target="tpu_custom_call" | custom-call | flops 2000000000 | bytes 1000000 | tf_op jit(solution)/shard_map/pallas_call | solution.py:88
  36.5 0.5 %collective-permute-start.5 = (f32[512,128]{1,0:T(8,128)S(1)}, f32[512,128]{1,0:T(8,128)S(1)}, u32[]{:S(2)}, u32[]{:S(2)}) collective-permute-start(f32[512,128]{1,0:T(8,128)S(1)} %shard_map.45), channel_id=1, source_target_pairs={{0,4},{4,0},{8,12},{12,8},{16,20},{20,16},{24,28},{28,24},{1,5},{5... | collective-permute-start | bytes 786440 | tf_op jit(solution)/shard_map/ppermute | solution.py:239
  37.0 0.8 %collective-permute-start.7 = (f32[512,128]{1,0:T(8,128)S(1)}, f32[512,128]{1,0:T(8,128)S(1)}, u32[]{:S(2)}, u32[]{:S(2)}) collective-permute-start(f32[512,128]{1,0:T(8,128)S(1)} %shard_map.42), channel_id=1, source_target_pairs={{0,16},{4,20},{8,24},{12,28},{16,0},{20,4},{24,8},{28,12},{1,17},{... | collective-permute-start | bytes 786440 | tf_op jit(solution)/shard_map/ppermute | solution.py:265
  37.9 0.0 collective-permute-done.4.refs_0_
  37.9 1.0 %shard_map.44 = f32[512,128]{1,0:T(8,128)S(1)} custom-call(f32[3,4,2,16,512]{4,3,2,1,0:T(8,128)S(1)} %get-tuple-element.26.left_ref, f32[3,3,32,512]{3,2,1,0:T(8,128)S(1)} %get-tuple-element.22.grad_ref, bf16[3,512,256]{2,1,0:T(8,128)(2,1)S(1)} %get-tuple-element.23.right_ref, f32[512,128]{1,0:T(8,128)S(1)} %collective-permute-done.4.refs_0_), custom_call_target="tpu_custom_call" | custom-call | flops 2000000000 | bytes 1000000 | tf_op jit(solution)/shard_map/pallas_call | solution.py:88
  38.9 0.9 %collective-permute-start.8 = (f32[512,128]{1,0:T(8,128)S(1)}, f32[512,128]{1,0:T(8,128)S(1)}, u32[]{:S(2)}, u32[]{:S(2)}) collective-permute-start(f32[512,128]{1,0:T(8,128)S(1)} %shard_map.44), channel_id=1, source_target_pairs={{0,8},{4,12},{8,0},{12,4},{16,24},{20,28},{24,16},{28,20},{1,9},{5... | collective-permute-start | bytes 786440 | tf_op jit(solution)/shard_map/ppermute | solution.py:265
  39.7 0.2 collective-permute-done.6.refs_1_
  40.0 0.0 collective-permute-done.5.refs_0_
  40.0 1.0 %shard_map.46 = f32[512,128]{1,0:T(8,128)S(1)} custom-call(f32[3,4,2,16,512]{4,3,2,1,0:T(8,128)S(1)} %get-tuple-element.26.left_ref, f32[3,3,32,512]{3,2,1,0:T(8,128)S(1)} %get-tuple-element.22.grad_ref, bf16[3,512,256]{2,1,0:T(8,128)(2,1)S(1)} %get-tuple-element.23.right_ref, f32[512,128]{1,0:T(8,128)S(1)} %collective-permute-done.5.refs_0_, ...), custom_call_target="tpu_custom_call" | custom-call | flops 2000000000 | bytes 1000000 | tf_op jit(solution)/shard_map/pallas_call | solution.py:88
  41.0 4.9 %collective-permute-done.7 = f32[512,128]{1,0:T(8,128)S(1)} collective-permute-done((f32[512,128]{1,0:T(8,128)S(1)}, f32[512,128]{1,0:T(8,128)S(1)}, u32[]{:S(2)}, u32[]{:S(2)}) %collective-permute-start.7) | collective-permute-done | bytes 262176 | tf_op jit(solution)/shard_map/ppermute | solution.py:265
  45.9 1.1 %collective-permute-done.8 = f32[512,128]{1,0:T(8,128)S(1)} collective-permute-done((f32[512,128]{1,0:T(8,128)S(1)}, f32[512,128]{1,0:T(8,128)S(1)}, u32[]{:S(2)}, u32[]{:S(2)}) %collective-permute-start.8) | collective-permute-done | bytes 262176 | tf_op jit(solution)/shard_map/ppermute | solution.py:265
  46.9 0.8 %add_add_fusion = f32[512,128]{1,0:T(8,128)} fusion(f32[512,128]{1,0:T(8,128)S(1)} %collective-permute-done.8, f32[512,128]{1,0:T(8,128)S(1)} %shard_map.46, f32[512,128]{1,0:T(8,128)S(1)} %collective-permute-done.7), kind=kLoop, calls=%fused_computation | loop fusion | flops 131072 | bytes 1048576 | tf_op jit(solution)/shard_map/add | solution.py:277
Async XLA Ops:
  0.0 0.9 %copy-start = (f32[3,32,1,512]{3,2,1,0:T(1,128)S(1)}, f32[3,32,1,512]{3,2,1,0:T(1,128)}, u32[]{:S(2)}) copy-start(f32[3,32,1,512]{3,2,1,0:T(1,128)} %param.3) | copy-start | bytes 589828
  1.1 20.5 %collective-permute-start = (f32[96,128]{1,0:T(8,128)S(1)}, f32[96,128]{1,0:T(8,128)S(1)}, u32[]{:S(2)}, u32[]{:S(2)}) collective-permute-start(f32[96,128]{1,0:T(8,128)S(1)} %get-tuple-element.16), channel_id=1, source_target_pairs={{0,4},{4,0},{8,12},{12,8},{16,20},{20,16},{24,28},{28,24},{1,5},{5... | collective-permute-start | bytes 147464 | tf_op jit(solution)/shard_map/ppermute | solution.py:239
  1.6 20.0 %collective-permute-start.1 = (f32[96,128]{1,0:T(8,128)S(1)}, f32[96,128]{1,0:T(8,128)S(1)}, u32[]{:S(2)}, u32[]{:S(2)}) collective-permute-start(f32[96,128]{1,0:T(8,128)S(1)} %get-tuple-element.17), channel_id=1, source_target_pairs={{4,8},{12,16},{20,24},{8,4},{16,12},{24,20},{5,9},{13,17},{21,25},... | collective-permute-start | bytes 147464 | tf_op jit(solution)/shard_map/ppermute | solution.py:244
  2.3 19.3 %copy-start.2 = (s32[1,512]{1,0:T(1,128)S(1)}, s32[1,512]{1,0:T(1,128)}, u32[]{:S(2)}) copy-start(s32[1,512]{1,0:T(1,128)} %param.5) | copy-start | bytes 6148
  21.6 0.7 %copy-start.1 = (f32[1,512]{1,0:T(1,128)S(1)}, f32[1,512]{1,0:T(1,128)}, u32[]{:S(2)}) copy-start(f32[1,512]{1,0:T(1,128)} %param.4) | copy-start | bytes 6148
  25.0 2.8 %collective-permute-start.2 = (f32[512,128]{1,0:T(8,128)S(1)}, f32[512,128]{1,0:T(8,128)S(1)}, u32[]{:S(2)}, u32[]{:S(2)}) collective-permute-start(f32[512,128]{1,0:T(8,128)S(1)} %shard_map.39), channel_id=1, source_target_pairs={{0,4},{4,0},{8,12},{12,8},{16,20},{20,16},{24,28},{28,24},{1,5},{5... | collective-permute-start | bytes 786440 | tf_op jit(solution)/shard_map/ppermute | solution.py:239
  27.7 6.8 %collective-permute-start.3 = (f32[512,128]{1,0:T(8,128)S(1)}, f32[512,128]{1,0:T(8,128)S(1)}, u32[]{:S(2)}, u32[]{:S(2)}) collective-permute-start(f32[512,128]{1,0:T(8,128)S(1)} %shard_map.41), channel_id=1, source_target_pairs={{0,4},{4,0},{8,12},{12,8},{16,20},{20,16},{24,28},{28,24},{1,5},{5... | collective-permute-start | bytes 786440 | tf_op jit(solution)/shard_map/ppermute | solution.py:239
  28.8 11.1 %collective-permute-start.6 = (f32[512,128]{1,0:T(8,128)S(1)}, f32[512,128]{1,0:T(8,128)S(1)}, u32[]{:S(2)}, u32[]{:S(2)}) collective-permute-start(f32[512,128]{1,0:T(8,128)S(1)} %shard_map.40), channel_id=1, source_target_pairs={{0,24},{4,28},{8,16},{12,20},{16,8},{20,12},{24,0},{28,4},{1,25},{... | collective-permute-start | bytes 786440 | tf_op jit(solution)/shard_map/ppermute | solution.py:265
  34.4 3.5 %collective-permute-start.4 = (f32[512,128]{1,0:T(8,128)S(1)}, f32[512,128]{1,0:T(8,128)S(1)}, u32[]{:S(2)}, u32[]{:S(2)}) collective-permute-start(f32[512,128]{1,0:T(8,128)S(1)} %shard_map.43), channel_id=1, source_target_pairs={{0,4},{4,0},{8,12},{12,8},{16,20},{20,16},{24,28},{28,24},{1,5},{5... | collective-permute-start | bytes 786440 | tf_op jit(solution)/shard_map/ppermute | solution.py:239
  36.5 3.5 %collective-permute-start.5 = (f32[512,128]{1,0:T(8,128)S(1)}, f32[512,128]{1,0:T(8,128)S(1)}, u32[]{:S(2)}, u32[]{:S(2)}) collective-permute-start(f32[512,128]{1,0:T(8,128)S(1)} %shard_map.45), channel_id=1, source_target_pairs={{0,4},{4,0},{8,12},{12,8},{16,20},{20,16},{24,28},{28,24},{1,5},{5... | collective-permute-start | bytes 786440 | tf_op jit(solution)/shard_map/ppermute | solution.py:239
  37.0 8.9 %collective-permute-start.7 = (f32[512,128]{1,0:T(8,128)S(1)}, f32[512,128]{1,0:T(8,128)S(1)}, u32[]{:S(2)}, u32[]{:S(2)}) collective-permute-start(f32[512,128]{1,0:T(8,128)S(1)} %shard_map.42), channel_id=1, source_target_pairs={{0,16},{4,20},{8,24},{12,28},{16,0},{20,4},{24,8},{28,12},{1,17},{... | collective-permute-start | bytes 786440 | tf_op jit(solution)/shard_map/ppermute | solution.py:265
  38.9 8.1 %collective-permute-start.8 = (f32[512,128]{1,0:T(8,128)S(1)}, f32[512,128]{1,0:T(8,128)S(1)}, u32[]{:S(2)}, u32[]{:S(2)}) collective-permute-start(f32[512,128]{1,0:T(8,128)S(1)} %shard_map.44), channel_id=1, source_target_pairs={{0,8},{4,12},{8,0},{12,4},{16,24},{20,28},{24,16},{28,20},{1,9},{5... | collective-permute-start | bytes 786440 | tf_op jit(solution)/shard_map/ppermute | solution.py:265

commit v3 on v2

--- a/solution.py
+++ b/solution.py
@@ -103,7 +103,7 @@
     return lax.broadcasted_iota(jnp.int32, (rows, LANES), 1)
 
 
-def rim_kernel(own_ref, inner_ref, outer_ref):
+def rim_kernel(own_ref, volume_ref, mask_ref, inner_ref, outer_ref, weights_ref):
     rows = inner_ref.shape[0]
     upper = lax.axis_index("space") % 2 == 1
     lane = lane_index(rows)
@@ -115,11 +115,12 @@
         inside = (lane >= width * x) & (lane < width * (x + 1))
         firsts = jnp.where(inside, pltpu.roll(chunk, (width * x) % LANES, 1), firsts)
         lasts = jnp.where(inside, pltpu.roll(chunk, (width * x + width) % LANES, 1), lasts)
+    weights_ref[...] = volume_ref[...] * mask_ref[...].astype(F32)
     inner_ref[...] = jnp.where(upper, firsts, lasts)
     outer_ref[...] = jnp.where(upper, lasts, firsts)
 
 
-def write_gradient(own_ref, inner_ref, outer_ref, grad_ref):
+def gradient_kernel(own_ref, inner_ref, outer_ref, grad_ref):
     k_count = grad_ref.shape[2]
     upper = lax.axis_index("space") % 2 == 1
     lane = lane_index(k_count)
@@ -168,18 +169,37 @@
     return high, (value - high.astype(F32)).astype(BF16)
 
 
-def prepare_kernel(
-    fields_hbm, own_ref, inner_ref, outer_ref, volume_ref, mask_ref, grad_ref, right_ref, left_ref, fields_ref, arrived
+def assemble_kernel(
+    own_ref, early_ref, late_ref, middle_ref, even_end_ref, odd_end_ref, weights_ref, right_ref, left_ref, fields_ref
 ):
-    copy = pltpu.make_async_copy(fields_hbm, fields_ref, arrived)
-    copy.start()
-    write_gradient(own_ref, inner_ref, outer_ref, grad_ref)
-    copy.wait()
+    odd = lax.axis_index("space") % 2 == 1
+    place = lax.axis_index("mode")
+    middle = (place == 1) | (place == 2)
+    fields_ref[place] = own_ref[...]
+    fields_ref[jnp.where(odd, place ^ 1, place ^ 2)] = early_ref[...]
+    fields_ref[jnp.where(odd, place ^ 2, place ^ 1)] = late_ref[...]
+
+    @pl.when(middle)
+    def _():
+        fields_ref[place ^ 3] = middle_ref[...]
+
+    @pl.when(jnp.logical_not(middle) & odd)
+    def _():
+        fields_ref[place ^ 3] = odd_end_ref[...]
+
+    @pl.when(jnp.logical_not(middle) & jnp.logical_not(odd))
+    def _():
+        fields_ref[place ^ 3] = even_end_ref[...]
+
+    place_fields(fields_ref, weights_ref, right_ref, left_ref)
+
+
+def place_fields(fields_ref, weights_ref, right_ref, left_ref):
     blocks, block = fields_ref.shape[:2]
     k_count = block // (3 * TX)
     modes = blocks * k_count
     chips, cores, shares = left_ref.shape[1:4]
-    weights = volume_ref[...] * mask_ref[...].astype(F32)
+    weights = weights_ref[...]
     for d in range(3):
         for x in range(TX):
             cells = pl.ds(x * LANES, LANES)
@@ -238,22 +258,42 @@
     def swap(value):
         return lax.ppermute(value, "space", [(s, s ^ 1) for s in range(tiles)])
 
-    fields = lax.all_gather(own, "mode", axis=0, tiled=False)
-    inner, outer = on_chip(rim_kernel, [jax.ShapeDtypeStruct((3 * k_count, LANES), F32)] * 2)(own)
+    def along(value, even, odd):
+        pairs = [
+            (s * places + a, s * places + b) for s in range(tiles) for a, b in (odd if s % 2 else even)
+        ]
+        return lax.ppermute(value, ("space", "mode"), pairs)
+
+    inner, outer, weights = on_chip(
+        rim_kernel,
+        [jax.ShapeDtypeStruct((3 * k_count, LANES), F32)] * 2 + [jax.ShapeDtypeStruct((TX, LANES), F32)],
+    )(own, volume.reshape(TX, LANES), fluid_mask.reshape(TX, LANES))
     beyond = [(s, s + 1) for s in range(1, tiles - 1, 2)]
     outer = lax.ppermute(outer, "space", beyond + [(b, a) for a, b in beyond])
     inner = swap(inner)
-    fields, inner, outer = lax.optimization_barrier((fields, inner, outer))
-    gradient, right, left = on_chip(
-        prepare_kernel,
+
+    beside = [(place, place ^ 1) for place in range(places)]
+    across = [(place, place ^ 2) for place in range(places)]
+    centre, ends = [(1, 2), (2, 1)], [(1, 0), (2, 3)]
+    early = along(own, across, beside)
+    late = along(own, beside, across)
+    early, inner, outer = lax.optimization_barrier((early, inner, outer))
+    even_end = along(early, ends, [])
+    mine, early = lax.optimization_barrier((own, early))
+    middle = along(mine, centre, centre)
+    odd_end = along(late, [], ends)
+
+    gradient = on_chip(
+        gradient_kernel, jax.ShapeDtypeStruct((3, 3, k_count, CELLS), F32)
+    )(own, inner, outer)
+    right, left = on_chip(
+        assemble_kernel,
         [
-            jax.ShapeDtypeStruct((3, 3, k_count, CELLS), F32),
             jax.ShapeDtypeStruct((3, CELLS, 2 * modes), BF16),
             jax.ShapeDtypeStruct((3, tiles // 2, 2, shares, CELLS), F32),
         ],
-        scratch=[pltpu.VMEM(fields.shape, F32), pltpu.SemaphoreType.DMA],
-        in_place=1,
-    )(fields, own, inner, outer, volume.reshape(TX, LANES), fluid_mask.reshape(TX, LANES))
+        scratch=[pltpu.VMEM((places, *own.shape), F32)],
+    )(own, early, late, middle, even_end, odd_end, weights)
 
     def term(apart, other, *given):
         return on_chip(

time: 47.9 us -> 44.8 us (0.935)
  blocking collectives: 19.3 us -> 0 us
  waiting for transfers between devices: 6.32 us -> 19 us
  starting transfers between devices: 9.8 us -> 13.8 us
  local copies, waits for them, and re-layouts: 1.6 us -> 0.96 us
    all_gather x1 -> x0, blocking collectives: 19.3 us -> none  [per_device_paired(): fields = lax.all_gather(own, 'mode', axis=0, tiled=False)]
    ppermute x0 -> x5, waiting for transfers between devices: none -> 12 us  [along(): return lax.ppermute(value, ('space', 'mode'), pairs)]
    ppermute x0 -> x5, starting transfers between devices: none -> 8.24 us  [along(): return lax.ppermute(value, ('space', 'mode'), pairs)]
    ppermute x3, starting transfers between devices: 6.25 us -> 3.63 us  [send(): lax.ppermute(value, 'space', [(s, s ^ 2 * apart) for s in range(tiles)])]
    ppermute x5, starting transfers between devices: 2.89 us -> 1.32 us  [swap(): return lax.ppermute(value, 'space', [(s, s ^ 1) for s in range(tiles)])]
    unnamed x6, local copies, waits for them, and re-layouts: 1.6 us -> 0.96 us
    pallas_call x10 -> x11, Pallas kernels: 9.84 us -> 9.87 us  [call(): pl.pallas_call(kernel, out_shape=out_shape, in_specs=[pl.BlockSpec(memory...]
  transfers between devices with their start and end apart: 9 -> 14, of which waited for: 4 -> 6; matrix products, arithmetic and copies ran while one was open for 0% -> 0% of each run, Pallas kernels for 15% -> 19%
where the time goes in v3:
time: 44.8 us; the launch traced here: 44.6 us
  waiting for transfers between devices  19 us (42%)
  starting transfers between devices  13.8 us (31%)
  Pallas kernels  9.87 us (22%)
  local copies, waits for them, and re-layouts  0.96 us (2%)
  other arithmetic  0.74 us (2%)
    ppermute x5, waiting for transfers between devices, along(): return lax.ppermute(value, ('space', 'mode'), pairs)  12 us
    pallas_call x11, Pallas kernels, call(): pl.pallas_call(kernel, out_shape=out_shape, in_specs=[pl.BlockSpec(memory...  9.87 us
    ppermute x5, starting transfers between devices, along(): return lax.ppermute(value, ('space', 'mode'), pairs)  8.24 us
    ppermute x3, waiting for transfers between devices, send(): lax.ppermute(value, 'space', [(s, s ^ 2 * apart) for s in range(tiles)])  6.46 us
    ppermute x3, starting transfers between devices, send(): lax.ppermute(value, 'space', [(s, s ^ 2 * apart) for s in range(tiles)])  3.63 us
    ppermute x5, starting transfers between devices, swap(): return lax.ppermute(value, 'space', [(s, s ^ 1) for s in range(tiles)])  1.32 us
    unnamed x6, local copies, waits for them, and re-layouts  0.96 us
  transfers between devices with their start and end apart: 14, of which 6 were waited for; matrix products, arithmetic and copies ran while one was open for 0% of the time, Pallas kernels for 19%

profile of v3, /device:TPU:0, one launch (start us, length us, event | category | flops | bytes accessed | tf_op | source)
XLA Modules:
  0.0 44.6 jit_solution(11580034514808932103)
XLA Ops:
  0.0 0.0 copy-start.2
  0.0 0.0 copy-start.1
  0.0 3.0 %collective-permute-start.3 = (f32[384,128]{1,0:T(8,128)}, f32[384,128]{1,0:T(8,128)S(1)}, u32[]{:S(2)}, u32[]{:S(2)}) collective-permute-start(f32[384,128]{1,0:T(8,128)} %bitcast.6), channel_id=1, source_target_pairs={{0,1},{1,0},{2,3},{3,2},{4,6},{5,7},{6,4},{7,5},{8,9},{9,8},{10,11... | collective-permute-start | bytes 589832 | tf_op jit(solution)/shard_map/ppermute | solution.py:265
  3.0 2.6 %collective-permute-start = (f32[384,128]{1,0:T(8,128)}, f32[384,128]{1,0:T(8,128)S(1)}, u32[]{:S(2)}, u32[]{:S(2)}) collective-permute-start(f32[384,128]{1,0:T(8,128)} %bitcast.7), channel_id=1, source_target_pairs={{0,2},{1,3},{2,0},{3,1},{4,5},{5,4},{6,7},{7,6},{8,10},{9,11},{10,... | collective-permute-start | bytes 589832 | tf_op jit(solution)/shard_map/ppermute | solution.py:265
  5.6 0.0 copy-done.2
  5.6 0.0 copy-done.1
  5.6 0.0 copy-start
  5.6 1.0 %copy-done = f32[3,32,1,512]{3,2,1,0:T(1,128)S(1)} copy-done((f32[3,32,1,512]{3,2,1,0:T(1,128)S(1)}, f32[3,32,1,512]{3,2,1,0:T(1,128)}, u32[]{:S(2)}) %copy-start) | copy-done | bytes 196632
  6.6 0.2 shard_map.37
  6.7 0.1 collective-permute-start.1
  6.8 0.7 %collective-permute-start.2 = (f32[96,128]{1,0:T(8,128)S(1)}, f32[96,128]{1,0:T(8,128)S(1)}, u32[]{:S(2)}, u32[]{:S(2)}) collective-permute-start(f32[96,128]{1,0:T(8,128)S(1)} %get-tuple-element.19), channel_id=1, source_target_pairs={{4,8},{12,16},{20,24},{8,4},{16,12},{24,20},{5,9},{13,17},{21,25},... | collective-permute-start | bytes 147464 | tf_op jit(solution)/shard_map/ppermute | solution.py:272
  7.5 0.5 %collective-permute-done.1.inner_ref = f32[96,128]{1,0:T(8,128)S(1)} collective-permute-done((f32[96,128]{1,0:T(8,128)S(1)}, f32[96,128]{1,0:T(8,128)S(1)}, u32[]{:S(2)}, u32[]{:S(2)}) %collective-permute-start.1) | collective-permute-done | bytes 49184 | tf_op jit(solution)/shard_map/ppermute | solution.py:259
  8.0 0.0 collective-permute-done.2.outer_ref
  8.0 4.7 %collective-permute-done.early_ref = f32[384,128]{1,0:T(8,128)S(1)} collective-permute-done((f32[384,128]{1,0:T(8,128)}, f32[384,128]{1,0:T(8,128)S(1)}, u32[]{:S(2)}, u32[]{:S(2)}) %collective-permute-start) | collective-permute-done | bytes 196640 | tf_op jit(solution)/shard_map/ppermute | solution.py:265
  12.7 0.0 collective-permute-done.3.late_ref
  12.7 0.7 %collective-permute-start.6 = (f32[384,128]{1,0:T(8,128)S(1)}, f32[384,128]{1,0:T(8,128)S(1)}, u32[]{:S(2)}, u32[]{:S(2)}) collective-permute-start(f32[384,128]{1,0:T(8,128)S(1)} %collective-permute-done.3.late_ref), channel_id=1, source_target_pairs={{5,4},{6,7},{13,12},{14,15},{21,20},{22,23},{29,28},{30,31}} | collective-permute-start | bytes 589832 | tf_op jit(solution)/shard_map/ppermute | solution.py:265
  13.4 0.7 %collective-permute-start.4 = (f32[384,128]{1,0:T(8,128)S(1)}, f32[384,128]{1,0:T(8,128)S(1)}, u32[]{:S(2)}, u32[]{:S(2)}) collective-permute-start(f32[384,128]{1,0:T(8,128)S(1)} %bitcast.9), channel_id=1, source_target_pairs={{1,2},{2,1},{5,6},{6,5},{9,10},{10,9},{13,14},{14,13},{17,18},{18,... | collective-permute-start | bytes 589832 | tf_op jit(solution)/shard_map/ppermute | solution.py:265
  14.1 1.3 %collective-permute-start.5 = (f32[384,128]{1,0:T(8,128)S(1)}, f32[384,128]{1,0:T(8,128)S(1)}, u32[]{:S(2)}, u32[]{:S(2)}) collective-permute-start(f32[384,128]{1,0:T(8,128)S(1)} %collective-permute-done.early_ref), channel_id=1, source_target_pairs={{1,0},{2,3},{9,8},{10,11},{17,16},{18,19},{25,24},{26,27}} | collective-permute-start | bytes 589832 | tf_op jit(solution)/shard_map/ppermute | solution.py:265
  15.4 1.4 %shard_map.39.grad_ref = f32[3,3,32,512]{3,2,1,0:T(8,128)S(1)} custom-call(f32[384,128]{1,0:T(8,128)S(1)} %bitcast.10, f32[96,128]{1,0:T(8,128)S(1)} %collective-permute-done.1.inner_ref, f32[96,128]{1,0:T(8,128)S(1)} %collective-permute-done.2.outer_ref), custom_call_target="tpu_custom_call" | custom-call | flops 2000000000 | bytes 1000000 | tf_op jit(solution)/shard_map/pallas_call | solution.py:88
  16.8 0.0 collective-permute-done.6.odd_end_ref
  16.8 0.0 collective-permute-done.4.middle_ref
  16.8 7.3 %collective-permute-done.5.even_end_ref = f32[384,128]{1,0:T(8,128)S(1)} collective-permute-done((f32[384,128]{1,0:T(8,128)S(1)}, f32[384,128]{1,0:T(8,128)S(1)}, u32[]{:S(2)}, u32[]{:S(2)}) %collective-permute-start.5) | collective-permute-done | bytes 196640 | tf_op jit(solution)/shard_map/ppermute | solution.py:265
  24.1 0.3 shard_map.38
  24.4 1.0 %shard_map.40 = f32[512,128]{1,0:T(8,128)S(1)} custom-call(f32[3,4,2,16,512]{4,3,2,1,0:T(8,128)S(1)} %get-tuple-element.30.left_ref, f32[3,3,32,512]{3,2,1,0:T(8,128)S(1)} %shard_map.39.grad_ref, bf16[3,512,256]{2,1,0:T(8,128)(2,1)S(1)} %get-tuple-element.27.right_ref), custom_call_target="tpu_custom_call" | custom-call | flops 2000000000 | bytes 1000000 | tf_op jit(solution)/shard_map/pallas_call | solution.py:88
  25.4 0.1 collective-permute-start.7
  25.5 1.0 %shard_map.42 = f32[512,128]{1,0:T(8,128)S(1)} custom-call(f32[3,4,2,16,512]{4,3,2,1,0:T(8,128)S(1)} %get-tuple-element.30.left_ref, f32[3,3,32,512]{3,2,1,0:T(8,128)S(1)} %shard_map.39.grad_ref, bf16[3,512,256]{2,1,0:T(8,128)(2,1)S(1)} %get-tuple-element.27.right_ref), custom_call_target="tpu_custom_call" | custom-call | flops 2000000000 | bytes 1000000 | tf_op jit(solution)/shard_map/pallas_call | solution.py:88
  26.5 0.6 %collective-permute-start.8 = (f32[512,128]{1,0:T(8,128)S(1)}, f32[512,128]{1,0:T(8,128)S(1)}, u32[]{:S(2)}, u32[]{:S(2)}) collective-permute-start(f32[512,128]{1,0:T(8,128)S(1)} %shard_map.42), channel_id=1, source_target_pairs={{0,4},{4,0},{8,12},{12,8},{16,20},{20,16},{24,28},{28,24},{1,5},{5... | collective-permute-start | bytes 786440 | tf_op jit(solution)/shard_map/ppermute | solution.py:259
  27.1 0.0 collective-permute-done.7.refs_0_
  27.1 1.0 %shard_map.41 = f32[512,128]{1,0:T(8,128)S(1)} custom-call(f32[3,4,2,16,512]{4,3,2,1,0:T(8,128)S(1)} %get-tuple-element.30.left_ref, f32[3,3,32,512]{3,2,1,0:T(8,128)S(1)} %shard_map.39.grad_ref, bf16[3,512,256]{2,1,0:T(8,128)(2,1)S(1)} %get-tuple-element.27.right_ref, f32[512,128]{1,0:T(8,128)S(1)} %collective-permute-done.7.refs_0_), custom_call_target="tpu_custom_call" | custom-call | flops 2000000000 | bytes 1000000 | tf_op jit(solution)/shard_map/pallas_call | solution.py:88
  28.1 2.5 %collective-permute-start.11 = (f32[512,128]{1,0:T(8,128)S(1)}, f32[512,128]{1,0:T(8,128)S(1)}, u32[]{:S(2)}, u32[]{:S(2)}) collective-permute-start(f32[512,128]{1,0:T(8,128)S(1)} %shard_map.41), channel_id=1, source_target_pairs={{0,24},{4,28},{8,16},{12,20},{16,8},{20,12},{24,0},{28,4},{1,25},{... | collective-permute-start | bytes 786440 | tf_op jit(solution)/shard_map/ppermute | solution.py:305
  30.6 1.0 %shard_map.44 = f32[512,128]{1,0:T(8,128)S(1)} custom-call(f32[3,4,2,16,512]{4,3,2,1,0:T(8,128)S(1)} %get-tuple-element.30.left_ref, f32[3,3,32,512]{3,2,1,0:T(8,128)S(1)} %shard_map.39.grad_ref, bf16[3,512,256]{2,1,0:T(8,128)(2,1)S(1)} %get-tuple-element.27.right_ref), custom_call_target="tpu_custom_call" | custom-call | flops 2000000000 | bytes 1000000 | tf_op jit(solution)/shard_map/pallas_call | solution.py:88
  31.6 0.1 collective-permute-start.9
  31.7 0.0 collective-permute-done.8.refs_0_
  31.7 1.0 %shard_map.43 = f32[512,128]{1,0:T(8,128)S(1)} custom-call(f32[3,4,2,16,512]{4,3,2,1,0:T(8,128)S(1)} %get-tuple-element.30.left_ref, f32[3,3,32,512]{3,2,1,0:T(8,128)S(1)} %shard_map.39.grad_ref, bf16[3,512,256]{2,1,0:T(8,128)(2,1)S(1)} %get-tuple-element.27.right_ref, f32[512,128]{1,0:T(8,128)S(1)} %collective-permute-done.8.refs_0_), custom_call_target="tpu_custom_call" | custom-call | flops 2000000000 | bytes 1000000 | tf_op jit(solution)/shard_map/pallas_call | solution.py:88
  32.7 1.0 %shard_map.46 = f32[512,128]{1,0:T(8,128)S(1)} custom-call(f32[3,4,2,16,512]{4,3,2,1,0:T(8,128)S(1)} %get-tuple-element.30.left_ref, f32[3,3,32,512]{3,2,1,0:T(8,128)S(1)} %shard_map.39.grad_ref, bf16[3,512,256]{2,1,0:T(8,128)(2,1)S(1)} %get-tuple-element.27.right_ref), custom_call_target="tpu_custom_call" | custom-call | flops 2000000000 | bytes 1000000 | tf_op jit(solution)/shard_map/pallas_call | solution.py:88
  33.7 0.5 %collective-permute-start.10 = (f32[512,128]{1,0:T(8,128)S(1)}, f32[512,128]{1,0:T(8,128)S(1)}, u32[]{:S(2)}, u32[]{:S(2)}) collective-permute-start(f32[512,128]{1,0:T(8,128)S(1)} %shard_map.46), channel_id=1, source_target_pairs={{0,4},{4,0},{8,12},{12,8},{16,20},{20,16},{24,28},{28,24},{1,5},{5... | collective-permute-start | bytes 786440 | tf_op jit(solution)/shard_map/ppermute | solution.py:259
  34.2 0.5 %collective-permute-start.12 = (f32[512,128]{1,0:T(8,128)S(1)}, f32[512,128]{1,0:T(8,128)S(1)}, u32[]{:S(2)}, u32[]{:S(2)}) collective-permute-start(f32[512,128]{1,0:T(8,128)S(1)} %shard_map.43), channel_id=1, source_target_pairs={{0,16},{4,20},{8,24},{12,28},{16,0},{20,4},{24,8},{28,12},{1,17},{... | collective-permute-start | bytes 786440 | tf_op jit(solution)/shard_map/ppermute | solution.py:305
  34.8 0.0 collective-permute-done.9.refs_0_
  34.8 1.0 %shard_map.45 = f32[512,128]{1,0:T(8,128)S(1)} custom-call(f32[3,4,2,16,512]{4,3,2,1,0:T(8,128)S(1)} %get-tuple-element.30.left_ref, f32[3,3,32,512]{3,2,1,0:T(8,128)S(1)} %shard_map.39.grad_ref, bf16[3,512,256]{2,1,0:T(8,128)(2,1)S(1)} %get-tuple-element.27.right_ref, f32[512,128]{1,0:T(8,128)S(1)} %collective-permute-done.9.refs_0_), custom_call_target="tpu_custom_call" | custom-call | flops 2000000000 | bytes 1000000 | tf_op jit(solution)/shard_map/pallas_call | solution.py:88
  35.8 0.6 %collective-permute-start.13 = (f32[512,128]{1,0:T(8,128)S(1)}, f32[512,128]{1,0:T(8,128)S(1)}, u32[]{:S(2)}, u32[]{:S(2)}) collective-permute-start(f32[512,128]{1,0:T(8,128)S(1)} %shard_map.45), channel_id=1, source_target_pairs={{0,8},{4,12},{8,0},{12,4},{16,24},{20,28},{24,16},{28,20},{1,9},{5... | collective-permute-start | bytes 786440 | tf_op jit(solution)/shard_map/ppermute | solution.py:305
  36.4 1.0 %collective-permute-done.11.refs_1_ = f32[512,128]{1,0:T(8,128)S(1)} collective-permute-done((f32[512,128]{1,0:T(8,128)S(1)}, f32[512,128]{1,0:T(8,128)S(1)}, u32[]{:S(2)}, u32[]{:S(2)}) %collective-permute-start.11) | collective-permute-done | bytes 262176 | tf_op jit(solution)/shard_map/ppermute | solution.py:305
  37.4 0.0 collective-permute-done.10.refs_0_
  37.4 1.0 %shard_map.47 = f32[512,128]{1,0:T(8,128)S(1)} custom-call(f32[3,4,2,16,512]{4,3,2,1,0:T(8,128)S(1)} %get-tuple-element.30.left_ref, f32[3,3,32,512]{3,2,1,0:T(8,128)S(1)} %shard_map.39.grad_ref, bf16[3,512,256]{2,1,0:T(8,128)(2,1)S(1)} %get-tuple-element.27.right_ref, f32[512,128]{1,0:T(8,128)S(1)} %collective-permute-done.10.refs_0_, ...), custom_call_target="tpu_custom_call" | custom-call | flops 2000000000 | bytes 1000000 | tf_op jit(solution)/shard_map/pallas_call | solution.py:88
  38.4 4.6 %collective-permute-done.12 = f32[512,128]{1,0:T(8,128)S(1)} collective-permute-done((f32[512,128]{1,0:T(8,128)S(1)}, f32[512,128]{1,0:T(8,128)S(1)}, u32[]{:S(2)}, u32[]{:S(2)}) %collective-permute-start.12) | collective-permute-done | bytes 262176 | tf_op jit(solution)/shard_map/ppermute | solution.py:305
  43.0 0.9 %collective-permute-done.13 = f32[512,128]{1,0:T(8,128)S(1)} collective-permute-done((f32[512,128]{1,0:T(8,128)S(1)}, f32[512,128]{1,0:T(8,128)S(1)}, u32[]{:S(2)}, u32[]{:S(2)}) %collective-permute-start.13) | collective-permute-done | bytes 262176 | tf_op jit(solution)/shard_map/ppermute | solution.py:305
  43.9 0.7 %add_add_fusion = f32[512,128]{1,0:T(8,128)} fusion(f32[512,128]{1,0:T(8,128)S(1)} %collective-permute-done.13, f32[512,128]{1,0:T(8,128)S(1)} %shard_map.47, f32[512,128]{1,0:T(8,128)S(1)} %collective-permute-done.12), kind=kLoop, calls=%fused_computation | loop fusion | flops 131072 | bytes 1048576 | tf_op jit(solution)/shard_map/add | solution.py:317
Async XLA Ops:
  0.0 5.6 %copy-start.2 = (s32[1,512]{1,0:T(1,128)S(1)}, s32[1,512]{1,0:T(1,128)}, u32[]{:S(2)}) copy-start(s32[1,512]{1,0:T(1,128)} %param.5) | copy-start | bytes 6148
  0.0 5.6 %copy-start.1 = (f32[1,512]{1,0:T(1,128)S(1)}, f32[1,512]{1,0:T(1,128)}, u32[]{:S(2)}) copy-start(f32[1,512]{1,0:T(1,128)} %param.4) | copy-start | bytes 6148
  0.0 12.7 %collective-permute-start.3 = (f32[384,128]{1,0:T(8,128)}, f32[384,128]{1,0:T(8,128)S(1)}, u32[]{:S(2)}, u32[]{:S(2)}) collective-permute-start(f32[384,128]{1,0:T(8,128)} %bitcast.6), channel_id=1, source_target_pairs={{0,1},{1,0},{2,3},{3,2},{4,6},{5,7},{6,4},{7,5},{8,9},{9,8},{10,11... | collective-permute-start | bytes 589832 | tf_op jit(solution)/shard_map/ppermute | solution.py:265
  3.0 9.7 %collective-permute-start = (f32[384,128]{1,0:T(8,128)}, f32[384,128]{1,0:T(8,128)S(1)}, u32[]{:S(2)}, u32[]{:S(2)}) collective-permute-start(f32[384,128]{1,0:T(8,128)} %bitcast.7), channel_id=1, source_target_pairs={{0,2},{1,3},{2,0},{3,1},{4,5},{5,4},{6,7},{7,6},{8,10},{9,11},{10,... | collective-permute-start | bytes 589832 | tf_op jit(solution)/shard_map/ppermute | solution.py:265
  5.6 1.0 %copy-start = (f32[3,32,1,512]{3,2,1,0:T(1,128)S(1)}, f32[3,32,1,512]{3,2,1,0:T(1,128)}, u32[]{:S(2)}) copy-start(f32[3,32,1,512]{3,2,1,0:T(1,128)} %param.3) | copy-start | bytes 589828
  6.7 1.3 %collective-permute-start.1 = (f32[96,128]{1,0:T(8,128)S(1)}, f32[96,128]{1,0:T(8,128)S(1)}, u32[]{:S(2)}, u32[]{:S(2)}) collective-permute-start(f32[96,128]{1,0:T(8,128)S(1)} %get-tuple-element.18), channel_id=1, source_target_pairs={{0,4},{4,0},{8,12},{12,8},{16,20},{20,16},{24,28},{28,24},{1,5},{5... | collective-permute-start | bytes 147464 | tf_op jit(solution)/shard_map/ppermute | solution.py:259
  6.8 1.2 %collective-permute-start.2 = (f32[96,128]{1,0:T(8,128)S(1)}, f32[96,128]{1,0:T(8,128)S(1)}, u32[]{:S(2)}, u32[]{:S(2)}) collective-permute-start(f32[96,128]{1,0:T(8,128)S(1)} %get-tuple-element.19), channel_id=1, source_target_pairs={{4,8},{12,16},{20,24},{8,4},{16,12},{24,20},{5,9},{13,17},{21,25},... | collective-permute-start | bytes 147464 | tf_op jit(solution)/shard_map/ppermute | solution.py:272
  12.7 4.0 %collective-permute-start.6 = (f32[384,128]{1,0:T(8,128)S(1)}, f32[384,128]{1,0:T(8,128)S(1)}, u32[]{:S(2)}, u32[]{:S(2)}) collective-permute-start(f32[384,128]{1,0:T(8,128)S(1)} %collective-permute-done.3.late_ref), channel_id=1, source_target_pairs={{5,4},{6,7},{13,12},{14,15},{21,20},{22,23},{29,28},{30,31}} | collective-permute-start | bytes 589832 | tf_op jit(solution)/shard_map/ppermute | solution.py:265
  13.4 3.4 %collective-permute-start.4 = (f32[384,128]{1,0:T(8,128)S(1)}, f32[384,128]{1,0:T(8,128)S(1)}, u32[]{:S(2)}, u32[]{:S(2)}) collective-permute-start(f32[384,128]{1,0:T(8,128)S(1)} %bitcast.9), channel_id=1, source_target_pairs={{1,2},{2,1},{5,6},{6,5},{9,10},{10,9},{13,14},{14,13},{17,18},{18,... | collective-permute-start | bytes 589832 | tf_op jit(solution)/shard_map/ppermute | solution.py:265
  14.1 10.0 %collective-permute-start.5 = (f32[384,128]{1,0:T(8,128)S(1)}, f32[384,128]{1,0:T(8,128)S(1)}, u32[]{:S(2)}, u32[]{:S(2)}) collective-permute-start(f32[384,128]{1,0:T(8,128)S(1)} %collective-permute-done.early_ref), channel_id=1, source_target_pairs={{1,0},{2,3},{9,8},{10,11},{17,16},{18,19},{25,24},{26,27}} | collective-permute-start | bytes 589832 | tf_op jit(solution)/shard_map/ppermute | solution.py:265
  25.4 1.6 %collective-permute-start.7 = (f32[512,128]{1,0:T(8,128)S(1)}, f32[512,128]{1,0:T(8,128)S(1)}, u32[]{:S(2)}, u32[]{:S(2)}) collective-permute-start(f32[512,128]{1,0:T(8,128)S(1)} %shard_map.40), channel_id=1, source_target_pairs={{0,4},{4,0},{8,12},{12,8},{16,20},{20,16},{24,28},{28,24},{1,5},{5... | collective-permute-start | bytes 786440 | tf_op jit(solution)/shard_map/ppermute | solution.py:259
  26.5 5.2 %collective-permute-start.8 = (f32[512,128]{1,0:T(8,128)S(1)}, f32[512,128]{1,0:T(8,128)S(1)}, u32[]{:S(2)}, u32[]{:S(2)}) collective-permute-start(f32[512,128]{1,0:T(8,128)S(1)} %shard_map.42), channel_id=1, source_target_pairs={{0,4},{4,0},{8,12},{12,8},{16,20},{20,16},{24,28},{28,24},{1,5},{5... | collective-permute-start | bytes 786440 | tf_op jit(solution)/shard_map/ppermute | solution.py:259
  28.1 9.3 %collective-permute-start.11 = (f32[512,128]{1,0:T(8,128)S(1)}, f32[512,128]{1,0:T(8,128)S(1)}, u32[]{:S(2)}, u32[]{:S(2)}) collective-permute-start(f32[512,128]{1,0:T(8,128)S(1)} %shard_map.41), channel_id=1, source_target_pairs={{0,24},{4,28},{8,16},{12,20},{16,8},{20,12},{24,0},{28,4},{1,25},{... | collective-permute-start | bytes 786440 | tf_op jit(solution)/shard_map/ppermute | solution.py:305
  31.6 3.2 %collective-permute-start.9 = (f32[512,128]{1,0:T(8,128)S(1)}, f32[512,128]{1,0:T(8,128)S(1)}, u32[]{:S(2)}, u32[]{:S(2)}) collective-permute-start(f32[512,128]{1,0:T(8,128)S(1)} %shard_map.44), channel_id=1, source_target_pairs={{0,4},{4,0},{8,12},{12,8},{16,20},{20,16},{24,28},{28,24},{1,5},{5... | collective-permute-start | bytes 786440 | tf_op jit(solution)/shard_map/ppermute | solution.py:259
  33.7 3.7 %collective-permute-start.10 = (f32[512,128]{1,0:T(8,128)S(1)}, f32[512,128]{1,0:T(8,128)S(1)}, u32[]{:S(2)}, u32[]{:S(2)}) collective-permute-start(f32[512,128]{1,0:T(8,128)S(1)} %shard_map.46), channel_id=1, source_target_pairs={{0,4},{4,0},{8,12},{12,8},{16,20},{20,16},{24,28},{28,24},{1,5},{5... | collective-permute-start | bytes 786440 | tf_op jit(solution)/shard_map/ppermute | solution.py:259
  34.2 8.7 %collective-permute-start.12 = (f32[512,128]{1,0:T(8,128)S(1)}, f32[512,128]{1,0:T(8,128)S(1)}, u32[]{:S(2)}, u32[]{:S(2)}) collective-permute-start(f32[512,128]{1,0:T(8,128)S(1)} %shard_map.43), channel_id=1, source_target_pairs={{0,16},{4,20},{8,24},{12,28},{16,0},{20,4},{24,8},{28,12},{1,17},{... | collective-permute-start | bytes 786440 | tf_op jit(solution)/shard_map/ppermute | solution.py:305
  35.8 8.1 %collective-permute-start.13 = (f32[512,128]{1,0:T(8,128)S(1)}, f32[512,128]{1,0:T(8,128)S(1)}, u32[]{:S(2)}, u32[]{:S(2)}) collective-permute-start(f32[512,128]{1,0:T(8,128)S(1)} %shard_map.45), channel_id=1, source_target_pairs={{0,8},{4,12},{8,0},{12,4},{16,24},{20,28},{24,16},{28,20},{1,9},{5... | collective-permute-start | bytes 786440 | tf_op jit(solution)/shard_map/ppermute | solution.py:305

commit v4 on v3

--- a/solution.py
+++ b/solution.py
@@ -82,18 +82,17 @@
 MIB = 1 << 20
 
 
-def on_chip(kernel, out_shape, scratch=(), in_place=0, limit=48):
+def on_chip(kernel, out_shape, scratch=(), flops=2_000_000_000, limit=48):
 
     def call(*operands):
         return pl.pallas_call(
             kernel,
             out_shape=out_shape,
-            in_specs=[pl.BlockSpec(memory_space=pl.ANY)] * in_place
-            + [pl.BlockSpec(memory_space=pltpu.VMEM)] * (len(operands) - in_place),
+            in_specs=[pl.BlockSpec(memory_space=pltpu.VMEM)] * len(operands),
             out_specs=jax.tree.map(lambda _: pl.BlockSpec(memory_space=pltpu.VMEM), out_shape),
             scratch_shapes=list(scratch),
             compiler_params=pltpu.CompilerParams(vmem_limit_bytes=limit * MIB),
-            cost_estimate=pl.CostEstimate(flops=2_000_000_000, bytes_accessed=1_000_000, transcendentals=0),
+            cost_estimate=pl.CostEstimate(flops=flops, bytes_accessed=flops // 2000, transcendentals=0),
         )(*operands)
 
     return call
@@ -122,7 +121,9 @@
 
 def gradient_kernel(own_ref, inner_ref, outer_ref, grad_ref):
     k_count = grad_ref.shape[2]
-    upper = lax.axis_index("space") % 2 == 1
+    tile, tiles = lax.axis_index("space"), lax.axis_size("space")
+    upper = tile % 2 == 1
+    at_end = (tile == 0) | (tile == tiles - 1)
     lane = lane_index(k_count)
     in_z = lane % TZ
     width = 2 * TZ
@@ -139,7 +140,7 @@
     zero = jnp.zeros((k_count, LANES), F32)
     for d in range(3):
         rows = pl.ds(d * k_count, k_count)
-        inner, outer = inner_ref[rows, :], outer_ref[rows, :]
+        inner, outer = inner_ref[rows, :], jnp.where(at_end, 0.0, outer_ref[rows, :])
         rim_before = jnp.where(upper, inner, outer)
         rim_after = jnp.where(upper, outer, inner)
         own = [own_ref[pl.ds(d * k_count * TX + x, k_count, stride=TX), :] for x in range(TX)]
@@ -169,28 +170,11 @@
     return high, (value - high.astype(F32)).astype(BF16)
 
 
-def assemble_kernel(
-    own_ref, early_ref, late_ref, middle_ref, even_end_ref, odd_end_ref, weights_ref, right_ref, left_ref, fields_ref
-):
-    odd = lax.axis_index("space") % 2 == 1
+def assemble_kernel(*refs):
+    blocks, (weights_ref, right_ref, left_ref, fields_ref) = refs[:-4], refs[-4:]
     place = lax.axis_index("mode")
-    middle = (place == 1) | (place == 2)
-    fields_ref[place] = own_ref[...]
-    fields_ref[jnp.where(odd, place ^ 1, place ^ 2)] = early_ref[...]
-    fields_ref[jnp.where(odd, place ^ 2, place ^ 1)] = late_ref[...]
-
-    @pl.when(middle)
-    def _():
-        fields_ref[place ^ 3] = middle_ref[...]
-
-    @pl.when(jnp.logical_not(middle) & odd)
-    def _():
-        fields_ref[place ^ 3] = odd_end_ref[...]
-
-    @pl.when(jnp.logical_not(middle) & jnp.logical_not(odd))
-    def _():
-        fields_ref[place ^ 3] = even_end_ref[...]
-
+    for apart, block_ref in enumerate(blocks):
+        fields_ref[place ^ apart] = block_ref[...]
     place_fields(fields_ref, weights_ref, right_ref, left_ref)
 
 
@@ -258,34 +242,23 @@
     def swap(value):
         return lax.ppermute(value, "space", [(s, s ^ 1) for s in range(tiles)])
 
-    def along(value, even, odd):
-        pairs = [
-            (s * places + a, s * places + b) for s in range(tiles) for a, b in (odd if s % 2 else even)
-        ]
-        return lax.ppermute(value, ("space", "mode"), pairs)
-
     inner, outer, weights = on_chip(
         rim_kernel,
         [jax.ShapeDtypeStruct((3 * k_count, LANES), F32)] * 2 + [jax.ShapeDtypeStruct((TX, LANES), F32)],
+        flops=2000,
     )(own, volume.reshape(TX, LANES), fluid_mask.reshape(TX, LANES))
-    beyond = [(s, s + 1) for s in range(1, tiles - 1, 2)]
+    beyond = [(s, (s + 1) % tiles) for s in range(1, tiles, 2)]
     outer = lax.ppermute(outer, "space", beyond + [(b, a) for a, b in beyond])
     inner = swap(inner)
 
-    beside = [(place, place ^ 1) for place in range(places)]
-    across = [(place, place ^ 2) for place in range(places)]
-    centre, ends = [(1, 2), (2, 1)], [(1, 0), (2, 3)]
-    early = along(own, across, beside)
-    late = along(own, beside, across)
-    early, inner, outer = lax.optimization_barrier((early, inner, outer))
-    even_end = along(early, ends, [])
-    mine, early = lax.optimization_barrier((own, early))
-    middle = along(mine, centre, centre)
-    odd_end = along(late, [], ends)
+    blocks = [own]
+    for apart in range(1, places):
+        blocks.append(lax.ppermute(own, "mode", [(place, place ^ apart) for place in range(places)]))
 
     gradient = on_chip(
-        gradient_kernel, jax.ShapeDtypeStruct((3, 3, k_count, CELLS), F32)
+        gradient_kernel, jax.ShapeDtypeStruct((3, 3, k_count, CELLS), F32), flops=2000
     )(own, inner, outer)
+    weights, gradient = lax.optimization_barrier((weights, gradient))
     right, left = on_chip(
         assemble_kernel,
         [
@@ -293,7 +266,7 @@
             jax.ShapeDtypeStruct((3, tiles // 2, 2, shares, CELLS), F32),
         ],
         scratch=[pltpu.VMEM((places, *own.shape), F32)],
-    )(own, early, late, middle, even_end, odd_end, weights)
+    )(*blocks, weights)
 
     def term(apart, other, *given):
         return on_chip(

time: 44.8 us -> 42.6 us (0.951)
  waiting for transfers between devices: 19 us -> 17.5 us
  starting transfers between devices: 13.8 us -> 13.3 us
    ppermute x5 -> x3, waiting for transfers between devices: 12 us -> 9.2 us  [per_device_paired(): lax.ppermute(own, 'mode', [(place, place ^ apart) for place in range(plac...]
    ppermute x5 -> x3, starting transfers between devices: 8.24 us -> 5.69 us  [per_device_paired(): lax.ppermute(own, 'mode', [(place, place ^ apart) for place in range(plac...]
    ppermute x1, starting transfers between devices: 0.66 us -> 2.7 us  [per_device_paired(): outer = lax.ppermute(outer, 'space', beyond + [(b, a) for a, b in beyond])]
    ppermute x1, waiting for transfers between devices: 0.01 us -> 1.78 us  [per_device_paired(): outer = lax.ppermute(outer, 'space', beyond + [(b, a) for a, b in beyond])]
    ppermute x5, waiting for transfers between devices: 0.56 us -> 0.01 us  [swap(): return lax.ppermute(value, 'space', [(s, s ^ 1) for s in range(tiles)])]
  transfers between devices with their start and end apart: 14 -> 12, of which waited for: 6 -> 5; matrix products, arithmetic and copies ran while one was open for 0% -> 0% of each run, Pallas kernels for 19% -> 20%
where the time goes in v4:
time: 42.6 us; the launch traced here: 42.5 us
  waiting for transfers between devices  17.5 us (41%)
  starting transfers between devices  13.3 us (31%)
  Pallas kernels  9.86 us (23%)
  local copies, waits for them, and re-layouts  0.96 us (2%)
  other arithmetic  0.74 us (2%)
    pallas_call x11, Pallas kernels, call(): pl.pallas_call(kernel, out_shape=out_shape, in_specs=[pl.BlockSpec(memory...  9.86 us
    ppermute x3, waiting for transfers between devices, per_device_paired(): lax.ppermute(own, 'mode', [(place, place ^ apart) for place in range(plac...  9.2 us
    ppermute x3, waiting for transfers between devices, send(): lax.ppermute(value, 'space', [(s, s ^ 2 * apart) for s in range(tiles)])  6.47 us
    ppermute x3, starting transfers between devices, per_device_paired(): lax.ppermute(own, 'mode', [(place, place ^ apart) for place in range(plac...  5.69 us
    ppermute x3, starting transfers between devices, send(): lax.ppermute(value, 'space', [(s, s ^ 2 * apart) for s in range(tiles)])  3.62 us
    ppermute x1, starting transfers between devices, per_device_paired(): outer = lax.ppermute(outer, 'space', beyond + [(b, a) for a, b in beyond])  2.7 us
    ppermute x1, waiting for transfers between devices, per_device_paired(): outer = lax.ppermute(outer, 'space', beyond + [(b, a) for a, b in beyond])  1.78 us
    ppermute x5, starting transfers between devices, swap(): return lax.ppermute(value, 'space', [(s, s ^ 1) for s in range(tiles)])  1.32 us
  transfers between devices with their start and end apart: 12, of which 5 were waited for; matrix products, arithmetic and copies ran while one was open for 0% of the time, Pallas kernels for 20%

profile of v4, /device:TPU:0, one launch (start us, length us, event | category | flops | bytes accessed | tf_op | source)
XLA Modules:
  0.0 42.5 jit_solution(13796336049195358554)
XLA Ops:
  0.0 0.0 copy-start.2
  0.0 0.0 copy-start.1
  0.0 5.0 %collective-permute-start.2 = (f32[384,128]{1,0:T(8,128)}, f32[384,128]{1,0:T(8,128)S(1)}, u32[]{:S(2)}, u32[]{:S(2)}) collective-permute-start(f32[384,128]{1,0:T(8,128)} %bitcast.6), channel_id=1, source_target_pairs={{0,3},{1,2},{2,1},{3,0},{4,7},{5,6},{6,5},{7,4},{8,11},{9,10},{10,... | collective-permute-start | bytes 589832 | tf_op jit(solution)/shard_map/ppermute | solution.py:256
  5.1 0.0 collective-permute-start.1
  5.1 0.6 %collective-permute-start = (f32[384,128]{1,0:T(8,128)}, f32[384,128]{1,0:T(8,128)S(1)}, u32[]{:S(2)}, u32[]{:S(2)}) collective-permute-start(f32[384,128]{1,0:T(8,128)} %bitcast.8), channel_id=1, source_target_pairs={{0,1},{1,0},{2,3},{3,2},{4,5},{5,4},{6,7},{7,6},{8,9},{9,8},{10,11... | collective-permute-start | bytes 589832 | tf_op jit(solution)/shard_map/ppermute | solution.py:256
  5.7 0.0 copy-done.2
  5.7 0.0 copy-done.1
  5.7 0.0 copy-start
  5.7 1.0 %copy-done = f32[3,32,1,512]{3,2,1,0:T(1,128)S(1)} copy-done((f32[3,32,1,512]{3,2,1,0:T(1,128)S(1)}, f32[3,32,1,512]{3,2,1,0:T(1,128)}, u32[]{:S(2)}) %copy-start) | copy-done | bytes 196632
  6.7 0.2 shard_map.37
  6.8 0.1 collective-permute-start.3
  6.9 2.7 %collective-permute-start.4 = (f32[96,128]{1,0:T(8,128)S(1)}, f32[96,128]{1,0:T(8,128)S(1)}, u32[]{:S(2)}, u32[]{:S(2)}) collective-permute-start(f32[96,128]{1,0:T(8,128)S(1)} %get-tuple-element.17), channel_id=1, source_target_pairs={{4,8},{12,16},{20,24},{28,0},{8,4},{16,12},{24,20},{0,28},{5,9},{1... | collective-permute-start | bytes 147464 | tf_op jit(solution)/shard_map/ppermute | solution.py:251
  9.6 0.0 collective-permute-done.3.inner_ref
  9.6 1.8 %collective-permute-done.4.outer_ref = f32[96,128]{1,0:T(8,128)S(1)} collective-permute-done((f32[96,128]{1,0:T(8,128)S(1)}, f32[96,128]{1,0:T(8,128)S(1)}, u32[]{:S(2)}, u32[]{:S(2)}) %collective-permute-start.4) | collective-permute-done | bytes 49184 | tf_op jit(solution)/shard_map/ppermute | solution.py:251
  11.4 1.4 %shard_map.38.grad_ref = f32[3,3,32,512]{3,2,1,0:T(8,128)S(1)} custom-call(f32[384,128]{1,0:T(8,128)S(1)} %bitcast.10, f32[96,128]{1,0:T(8,128)S(1)} %collective-permute-done.3.inner_ref, f32[96,128]{1,0:T(8,128)S(1)} %collective-permute-done.4.outer_ref), custom_call_target="tpu_custom_call" | custom-call | flops 2000 | bytes 1 | tf_op jit(solution)/shard_map/pallas_call | solution.py:88
  12.8 0.0 collective-permute-done.2.refs_3_
  12.8 9.2 %collective-permute-done.1.refs_2_ = f32[384,128]{1,0:T(8,128)S(1)} collective-permute-done((f32[384,128]{1,0:T(8,128)}, f32[384,128]{1,0:T(8,128)S(1)}, u32[]{:S(2)}, u32[]{:S(2)}) %collective-permute-start.1) | collective-permute-done | bytes 196640 | tf_op jit(solution)/shard_map/ppermute | solution.py:256
  22.0 0.0 collective-permute-done.refs_1_
  22.0 0.3 shard_map.39
  22.3 1.0 %shard_map.40 = f32[512,128]{1,0:T(8,128)S(1)} custom-call(f32[3,4,2,16,512]{4,3,2,1,0:T(8,128)S(1)} %get-tuple-element.24.left_ref, f32[3,3,32,512]{3,2,1,0:T(8,128)S(1)} %shard_map.38.grad_ref, bf16[3,512,256]{2,1,0:T(8,128)(2,1)S(1)} %get-tuple-element.21.right_ref), custom_call_target="tpu_custom_call" | custom-call | flops 2000000000 | bytes 1000000 | tf_op jit(solution)/shard_map/pallas_call | solution.py:88
  23.3 0.1 collective-permute-start.5
  23.4 1.0 %shard_map.42 = f32[512,128]{1,0:T(8,128)S(1)} custom-call(f32[3,4,2,16,512]{4,3,2,1,0:T(8,128)S(1)} %get-tuple-element.24.left_ref, f32[3,3,32,512]{3,2,1,0:T(8,128)S(1)} %shard_map.38.grad_ref, bf16[3,512,256]{2,1,0:T(8,128)(2,1)S(1)} %get-tuple-element.21.right_ref), custom_call_target="tpu_custom_call" | custom-call | flops 2000000000 | bytes 1000000 | tf_op jit(solution)/shard_map/pallas_call | solution.py:88
  24.4 0.6 %collective-permute-start.6 = (f32[512,128]{1,0:T(8,128)S(1)}, f32[512,128]{1,0:T(8,128)S(1)}, u32[]{:S(2)}, u32[]{:S(2)}) collective-permute-start(f32[512,128]{1,0:T(8,128)S(1)} %shard_map.42), channel_id=1, source_target_pairs={{0,4},{4,0},{8,12},{12,8},{16,20},{20,16},{24,28},{28,24},{1,5},{5... | collective-permute-start | bytes 786440 | tf_op jit(solution)/shard_map/ppermute | solution.py:243
  24.9 0.0 collective-permute-done.5.refs_0_
  25.0 1.0 %shard_map.41 = f32[512,128]{1,0:T(8,128)S(1)} custom-call(f32[3,4,2,16,512]{4,3,2,1,0:T(8,128)S(1)} %get-tuple-element.24.left_ref, f32[3,3,32,512]{3,2,1,0:T(8,128)S(1)} %shard_map.38.grad_ref, bf16[3,512,256]{2,1,0:T(8,128)(2,1)S(1)} %get-tuple-element.21.right_ref, f32[512,128]{1,0:T(8,128)S(1)} %collective-permute-done.5.refs_0_), custom_call_target="tpu_custom_call" | custom-call | flops 2000000000 | bytes 1000000 | tf_op jit(solution)/shard_map/pallas_call | solution.py:88
  26.0 2.5 %collective-permute-start.9 = (f32[512,128]{1,0:T(8,128)S(1)}, f32[512,128]{1,0:T(8,128)S(1)}, u32[]{:S(2)}, u32[]{:S(2)}) collective-permute-start(f32[512,128]{1,0:T(8,128)S(1)} %shard_map.41), channel_id=1, source_target_pairs={{0,24},{4,28},{8,16},{12,20},{16,8},{20,12},{24,0},{28,4},{1,25},{... | collective-permute-start | bytes 786440 | tf_op jit(solution)/shard_map/ppermute | solution.py:278
  28.5 1.0 %shard_map.44 = f32[512,128]{1,0:T(8,128)S(1)} custom-call(f32[3,4,2,16,512]{4,3,2,1,0:T(8,128)S(1)} %get-tuple-element.24.left_ref, f32[3,3,32,512]{3,2,1,0:T(8,128)S(1)} %shard_map.38.grad_ref, bf16[3,512,256]{2,1,0:T(8,128)(2,1)S(1)} %get-tuple-element.21.right_ref), custom_call_target="tpu_custom_call" | custom-call | flops 2000000000 | bytes 1000000 | tf_op jit(solution)/shard_map/pallas_call | solution.py:88
  29.5 0.1 collective-permute-start.7
  29.6 0.0 collective-permute-done.6.refs_0_
  29.6 1.0 %shard_map.43 = f32[512,128]{1,0:T(8,128)S(1)} custom-call(f32[3,4,2,16,512]{4,3,2,1,0:T(8,128)S(1)} %get-tuple-element.24.left_ref, f32[3,3,32,512]{3,2,1,0:T(8,128)S(1)} %shard_map.38.grad_ref, bf16[3,512,256]{2,1,0:T(8,128)(2,1)S(1)} %get-tuple-element.21.right_ref, f32[512,128]{1,0:T(8,128)S(1)} %collective-permute-done.6.refs_0_), custom_call_target="tpu_custom_call" | custom-call | flops 2000000000 | bytes 1000000 | tf_op jit(solution)/shard_map/pallas_call | solution.py:88
  30.6 1.0 %shard_map.46 = f32[512,128]{1,0:T(8,128)S(1)} custom-call(f32[3,4,2,16,512]{4,3,2,1,0:T(8,128)S(1)} %get-tuple-element.24.left_ref, f32[3,3,32,512]{3,2,1,0:T(8,128)S(1)} %shard_map.38.grad_ref, bf16[3,512,256]{2,1,0:T(8,128)(2,1)S(1)} %get-tuple-element.21.right_ref), custom_call_target="tpu_custom_call" | custom-call | flops 2000000000 | bytes 1000000 | tf_op jit(solution)/shard_map/pallas_call | solution.py:88
  31.6 0.6 %collective-permute-start.8 = (f32[512,128]{1,0:T(8,128)S(1)}, f32[512,128]{1,0:T(8,128)S(1)}, u32[]{:S(2)}, u32[]{:S(2)}) collective-permute-start(f32[512,128]{1,0:T(8,128)S(1)} %shard_map.46), channel_id=1, source_target_pairs={{0,4},{4,0},{8,12},{12,8},{16,20},{20,16},{24,28},{28,24},{1,5},{5... | collective-permute-start | bytes 786440 | tf_op jit(solution)/shard_map/ppermute | solution.py:243
  32.1 0.5 %collective-permute-start.10 = (f32[512,128]{1,0:T(8,128)S(1)}, f32[512,128]{1,0:T(8,128)S(1)}, u32[]{:S(2)}, u32[]{:S(2)}) collective-permute-start(f32[512,128]{1,0:T(8,128)S(1)} %shard_map.43), channel_id=1, source_target_pairs={{0,16},{4,20},{8,24},{12,28},{16,0},{20,4},{24,8},{28,12},{1,17},{... | collective-permute-start | bytes 786440 | tf_op jit(solution)/shard_map/ppermute | solution.py:278
  32.6 0.0 collective-permute-done.7.refs_0_
  32.6 1.0 %shard_map.45 = f32[512,128]{1,0:T(8,128)S(1)} custom-call(f32[3,4,2,16,512]{4,3,2,1,0:T(8,128)S(1)} %get-tuple-element.24.left_ref, f32[3,3,32,512]{3,2,1,0:T(8,128)S(1)} %shard_map.38.grad_ref, bf16[3,512,256]{2,1,0:T(8,128)(2,1)S(1)} %get-tuple-element.21.right_ref, f32[512,128]{1,0:T(8,128)S(1)} %collective-permute-done.7.refs_0_), custom_call_target="tpu_custom_call" | custom-call | flops 2000000000 | bytes 1000000 | tf_op jit(solution)/shard_map/pallas_call | solution.py:88
  33.6 0.6 %collective-permute-start.11 = (f32[512,128]{1,0:T(8,128)S(1)}, f32[512,128]{1,0:T(8,128)S(1)}, u32[]{:S(2)}, u32[]{:S(2)}) collective-permute-start(f32[512,128]{1,0:T(8,128)S(1)} %shard_map.45), channel_id=1, source_target_pairs={{0,8},{4,12},{8,0},{12,4},{16,24},{20,28},{24,16},{28,20},{1,9},{5... | collective-permute-start | bytes 786440 | tf_op jit(solution)/shard_map/ppermute | solution.py:278
  34.2 1.0 %collective-permute-done.9.refs_1_ = f32[512,128]{1,0:T(8,128)S(1)} collective-permute-done((f32[512,128]{1,0:T(8,128)S(1)}, f32[512,128]{1,0:T(8,128)S(1)}, u32[]{:S(2)}, u32[]{:S(2)}) %collective-permute-start.9) | collective-permute-done | bytes 262176 | tf_op jit(solution)/shard_map/ppermute | solution.py:278
  35.3 0.0 collective-permute-done.8.refs_0_
  35.3 1.0 %shard_map.47 = f32[512,128]{1,0:T(8,128)S(1)} custom-call(f32[3,4,2,16,512]{4,3,2,1,0:T(8,128)S(1)} %get-tuple-element.24.left_ref, f32[3,3,32,512]{3,2,1,0:T(8,128)S(1)} %shard_map.38.grad_ref, bf16[3,512,256]{2,1,0:T(8,128)(2,1)S(1)} %get-tuple-element.21.right_ref, f32[512,128]{1,0:T(8,128)S(1)} %collective-permute-done.8.refs_0_, ...), custom_call_target="tpu_custom_call" | custom-call | flops 2000000000 | bytes 1000000 | tf_op jit(solution)/shard_map/pallas_call | solution.py:88
  36.3 4.6 %collective-permute-done.10 = f32[512,128]{1,0:T(8,128)S(1)} collective-permute-done((f32[512,128]{1,0:T(8,128)S(1)}, f32[512,128]{1,0:T(8,128)S(1)}, u32[]{:S(2)}, u32[]{:S(2)}) %collective-permute-start.10) | collective-permute-done | bytes 262176 | tf_op jit(solution)/shard_map/ppermute | solution.py:278
  40.8 0.9 %collective-permute-done.11 = f32[512,128]{1,0:T(8,128)S(1)} collective-permute-done((f32[512,128]{1,0:T(8,128)S(1)}, f32[512,128]{1,0:T(8,128)S(1)}, u32[]{:S(2)}, u32[]{:S(2)}) %collective-permute-start.11) | collective-permute-done | bytes 262176 | tf_op jit(solution)/shard_map/ppermute | solution.py:278
  41.7 0.7 %add_add_fusion = f32[512,128]{1,0:T(8,128)} fusion(f32[512,128]{1,0:T(8,128)S(1)} %collective-permute-done.11, f32[512,128]{1,0:T(8,128)S(1)} %shard_map.47, f32[512,128]{1,0:T(8,128)S(1)} %collective-permute-done.10), kind=kLoop, calls=%fused_computation | loop fusion | flops 131072 | bytes 1048576 | tf_op jit(solution)/shard_map/add | solution.py:290
Async XLA Ops:
  0.0 5.7 %copy-start.2 = (s32[1,512]{1,0:T(1,128)S(1)}, s32[1,512]{1,0:T(1,128)}, u32[]{:S(2)}) copy-start(s32[1,512]{1,0:T(1,128)} %param.5) | copy-start | bytes 6148
  0.0 5.7 %copy-start.1 = (f32[1,512]{1,0:T(1,128)S(1)}, f32[1,512]{1,0:T(1,128)}, u32[]{:S(2)}) copy-start(f32[1,512]{1,0:T(1,128)} %param.4) | copy-start | bytes 6148
  0.0 12.8 %collective-permute-start.2 = (f32[384,128]{1,0:T(8,128)}, f32[384,128]{1,0:T(8,128)S(1)}, u32[]{:S(2)}, u32[]{:S(2)}) collective-permute-start(f32[384,128]{1,0:T(8,128)} %bitcast.6), channel_id=1, source_target_pairs={{0,3},{1,2},{2,1},{3,0},{4,7},{5,6},{6,5},{7,4},{8,11},{9,10},{10,... | collective-permute-start | bytes 589832 | tf_op jit(solution)/shard_map/ppermute | solution.py:256
  5.1 16.9 %collective-permute-start.1 = (f32[384,128]{1,0:T(8,128)}, f32[384,128]{1,0:T(8,128)S(1)}, u32[]{:S(2)}, u32[]{:S(2)}) collective-permute-start(f32[384,128]{1,0:T(8,128)} %bitcast.7), channel_id=1, source_target_pairs={{0,2},{1,3},{2,0},{3,1},{4,6},{5,7},{6,4},{7,5},{8,10},{9,11},{10,... | collective-permute-start | bytes 589832 | tf_op jit(solution)/shard_map/ppermute | solution.py:256
  5.1 16.9 %collective-permute-start = (f32[384,128]{1,0:T(8,128)}, f32[384,128]{1,0:T(8,128)S(1)}, u32[]{:S(2)}, u32[]{:S(2)}) collective-permute-start(f32[384,128]{1,0:T(8,128)} %bitcast.8), channel_id=1, source_target_pairs={{0,1},{1,0},{2,3},{3,2},{4,5},{5,4},{6,7},{7,6},{8,9},{9,8},{10,11... | collective-permute-start | bytes 589832 | tf_op jit(solution)/shard_map/ppermute | solution.py:256
  5.7 1.0 %copy-start = (f32[3,32,1,512]{3,2,1,0:T(1,128)S(1)}, f32[3,32,1,512]{3,2,1,0:T(1,128)}, u32[]{:S(2)}) copy-start(f32[3,32,1,512]{3,2,1,0:T(1,128)} %param.3) | copy-start | bytes 589828
  6.8 2.8 %collective-permute-start.3 = (f32[96,128]{1,0:T(8,128)S(1)}, f32[96,128]{1,0:T(8,128)S(1)}, u32[]{:S(2)}, u32[]{:S(2)}) collective-permute-start(f32[96,128]{1,0:T(8,128)S(1)} %get-tuple-element.16), channel_id=1, source_target_pairs={{0,4},{4,0},{8,12},{12,8},{16,20},{20,16},{24,28},{28,24},{1,5},{5... | collective-permute-start | bytes 147464 | tf_op jit(solution)/shard_map/ppermute | solution.py:243
  6.9 4.5 %collective-permute-start.4 = (f32[96,128]{1,0:T(8,128)S(1)}, f32[96,128]{1,0:T(8,128)S(1)}, u32[]{:S(2)}, u32[]{:S(2)}) collective-permute-start(f32[96,128]{1,0:T(8,128)S(1)} %get-tuple-element.17), channel_id=1, source_target_pairs={{4,8},{12,16},{20,24},{28,0},{8,4},{16,12},{24,20},{0,28},{5,9},{1... | collective-permute-start | bytes 147464 | tf_op jit(solution)/shard_map/ppermute | solution.py:251
  23.3 1.6 %collective-permute-start.5 = (f32[512,128]{1,0:T(8,128)S(1)}, f32[512,128]{1,0:T(8,128)S(1)}, u32[]{:S(2)}, u32[]{:S(2)}) collective-permute-start(f32[512,128]{1,0:T(8,128)S(1)} %shard_map.40), channel_id=1, source_target_pairs={{0,4},{4,0},{8,12},{12,8},{16,20},{20,16},{24,28},{28,24},{1,5},{5... | collective-permute-start | bytes 786440 | tf_op jit(solution)/shard_map/ppermute | solution.py:243
  24.4 5.2 %collective-permute-start.6 = (f32[512,128]{1,0:T(8,128)S(1)}, f32[512,128]{1,0:T(8,128)S(1)}, u32[]{:S(2)}, u32[]{:S(2)}) collective-permute-start(f32[512,128]{1,0:T(8,128)S(1)} %shard_map.42), channel_id=1, source_target_pairs={{0,4},{4,0},{8,12},{12,8},{16,20},{20,16},{24,28},{28,24},{1,5},{5... | collective-permute-start | bytes 786440 | tf_op jit(solution)/shard_map/ppermute | solution.py:243
  26.0 9.3 %collective-permute-start.9 = (f32[512,128]{1,0:T(8,128)S(1)}, f32[512,128]{1,0:T(8,128)S(1)}, u32[]{:S(2)}, u32[]{:S(2)}) collective-permute-start(f32[512,128]{1,0:T(8,128)S(1)} %shard_map.41), channel_id=1, source_target_pairs={{0,24},{4,28},{8,16},{12,20},{16,8},{20,12},{24,0},{28,4},{1,25},{... | collective-permute-start | bytes 786440 | tf_op jit(solution)/shard_map/ppermute | solution.py:278
  29.5 3.2 %collective-permute-start.7 = (f32[512,128]{1,0:T(8,128)S(1)}, f32[512,128]{1,0:T(8,128)S(1)}, u32[]{:S(2)}, u32[]{:S(2)}) collective-permute-start(f32[512,128]{1,0:T(8,128)S(1)} %shard_map.44), channel_id=1, source_target_pairs={{0,4},{4,0},{8,12},{12,8},{16,20},{20,16},{24,28},{28,24},{1,5},{5... | collective-permute-start | bytes 786440 | tf_op jit(solution)/shard_map/ppermute | solution.py:243
  31.6 3.7 %collective-permute-start.8 = (f32[512,128]{1,0:T(8,128)S(1)}, f32[512,128]{1,0:T(8,128)S(1)}, u32[]{:S(2)}, u32[]{:S(2)}) collective-permute-start(f32[512,128]{1,0:T(8,128)S(1)} %shard_map.46), channel_id=1, source_target_pairs={{0,4},{4,0},{8,12},{12,8},{16,20},{20,16},{24,28},{28,24},{1,5},{5... | collective-permute-start | bytes 786440 | tf_op jit(solution)/shard_map/ppermute | solution.py:243
  32.1 8.7 %collective-permute-start.10 = (f32[512,128]{1,0:T(8,128)S(1)}, f32[512,128]{1,0:T(8,128)S(1)}, u32[]{:S(2)}, u32[]{:S(2)}) collective-permute-start(f32[512,128]{1,0:T(8,128)S(1)} %shard_map.43), channel_id=1, source_target_pairs={{0,16},{4,20},{8,24},{12,28},{16,0},{20,4},{24,8},{28,12},{1,17},{... | collective-permute-start | bytes 786440 | tf_op jit(solution)/shard_map/ppermute | solution.py:278
  33.6 8.1 %collective-permute-start.11 = (f32[512,128]{1,0:T(8,128)S(1)}, f32[512,128]{1,0:T(8,128)S(1)}, u32[]{:S(2)}, u32[]{:S(2)}) collective-permute-start(f32[512,128]{1,0:T(8,128)S(1)} %shard_map.45), channel_id=1, source_target_pairs={{0,8},{4,12},{8,0},{12,4},{16,24},{20,28},{24,16},{28,20},{1,9},{5... | collective-permute-start | bytes 786440 | tf_op jit(solution)/shard_map/ppermute | solution.py:278
